TPU v7x, 512 devices: a whole 4x8x8 slice. The times are simulated.
512 devices in a mesh: row: 32 (over y, x), col: 16 (over z, core).
Axes of the slice: x: 4, y: 8, z: 8, core: 2. Of those that a mesh axis runs over, the one named last changes fastest.
Arguments:
- positions: float32 [3, 16384], P(None, ('row', 'col')), may hold values from 0 to 1
- atom_types: int32 [16384], P(('row', 'col')), may hold values from 0 to 4
- alpha_table: float32 [5], replicated, may hold values from 0.2 to 0.6
- omega_table: float32 [5], replicated, may hold values from 0.4 to 1
- radius_table: float32 [5], replicated, may hold values from 0.8 to 1.2
- frequencies: float32 [8], replicated, may hold values from 0.05 to 0.8
- field: float32 [3, 8, 16384], P(None, None, ('row', 'col')), may hold values from -36 to 36
- start_dipoles: float32 [3, 8, 16384], P(None, None, ('row', 'col')), may hold values from -1.2 to 1.2
Outputs:
- dipoles: float32 [3, 8, 16384], P(None, None, ('row', 'col'))
- residual: float32 [3, 8, 16384], P(None, None, ('row', 'col'))
All inputs are finite; a program needn't handle non-finite values.
Results may differ from a plain program's by a relative error of at most 0.0003.
Values sent between devices are 32-bit elements; how exact they have to be, the bound alone decides.
A program may use at most 64 MiB of HBM per device.

v0:
```python
import jax
import jax.numpy as jnp
from jax import lax
from jax.sharding import PartitionSpec as P

ITERS = 3


PRECISE = lax.Precision.HIGHEST


def tensor_block(column_sites, row_sites):
    offsets = column_sites[:3, :, None] - row_sites[:3, None, :]
    reach = column_sites[3][:, None] + row_sites[3][None, :]
    square_dist = (
        offsets[0] * offsets[0] + offsets[1] * offsets[1] + offsets[2] * offsets[2] + reach * reach
    )
    inverse = lax.rsqrt(square_dist)
    inverse_cube = inverse * inverse * inverse
    inverse_fifth = inverse_cube * inverse * inverse
    identity = jnp.eye(3, dtype=jnp.float32)
    dyadic = -3.0 * offsets[:, None] * offsets[None, :] * inverse_fifth
    return dyadic + identity[:, :, None, None] * inverse_cube


def over_columns(width, step, carry):

    def turn(state, number):
        return (step(state, number * 128, 128), None)

    return lax.scan(turn, carry, jnp.arange(width // 128, dtype=jnp.int32))[0]


def shards(
    positions, atom_types, alpha_table, omega_table, radius_table, frequencies, field, start_dipoles
):
    piece = positions.shape[1]
    nfreq = frequencies.shape[0]
    row_count = lax.axis_size("row")
    column_count = lax.axis_size("col")
    row_atoms = piece * column_count
    side = (10.0 * piece * row_count * column_count) ** (1.0 / 3.0)
    row_index = lax.axis_index("row")
    column_index = lax.axis_index("col")
    lookup = (
        atom_types[None, :] == jnp.arange(alpha_table.shape[0], dtype=jnp.int32)[:, None]
    ).astype(jnp.float32)
    tables = jnp.stack([alpha_table, omega_table, radius_table])
    looked = jnp.dot(tables, lookup, precision=PRECISE)
    diagonal = (1.0 + (frequencies[:, None] / looked[1][None, :]) ** 2) / looked[0][None, :]
    local_sites = jnp.concatenate([positions * side, looked[2][None, :]], 0)
    row_sites = lax.all_gather(local_sites, "col", axis=1, tiled=True)
    row_labels = row_index * row_atoms + jnp.arange(row_atoms, dtype=jnp.int32)

    def column_labels(first, width):
        places = first + jnp.arange(width, dtype=jnp.int32)
        owners = places // piece
        return (owners, (owners * column_count + column_index) * piece + places % piece)

    def couple(vector):
        flat = vector.reshape(3 * nfreq, piece)
        initial = jnp.zeros((3 * nfreq, row_atoms), jnp.float32)
        column_sites = lax.all_gather(local_sites, "row", axis=1, tiled=True)
        column_vector = lax.all_gather(flat, "row", axis=1, tiled=True)

        def step(carry, offset, width):
            sites_part = lax.dynamic_slice_in_dim(column_sites, offset, width, 1)
            vector_part = lax.dynamic_slice_in_dim(column_vector, offset, width, 1).reshape(
                3, nfreq, width
            )
            owners, labels = column_labels(offset, width)
            kept = (labels[:, None] != row_labels[None, :]).astype(jnp.float32)
            tensor = tensor_block(sites_part, row_sites) * kept
            added = jnp.einsum("bfj,abji->afi", vector_part, tensor, precision=PRECISE)
            return carry + added.reshape(3 * nfreq, row_atoms)

        folded = over_columns(column_sites.shape[1], step, initial)
        result = lax.psum_scatter(folded, "col", scatter_dimension=1, tiled=True)
        return result.reshape(3, nfreq, piece)

    def apply(vector):
        return diagonal * vector + couple(vector)

    def local_inner(left, right):
        return jnp.sum(left * right, axis=(0, 2))

    dipoles = start_dipoles
    residual = field - apply(dipoles)

    def norm_of(values):
        return lax.psum(values, ("row", "col"))

    scaled = residual / diagonal
    direction = scaled
    norm_now = norm_of(local_inner(residual, scaled))
    for turn in range(ITERS):
        image = apply(direction)
        length = norm_now / lax.psum(local_inner(direction, image), ("row", "col"))
        dipoles = dipoles + length[None, :, None] * direction
        residual = residual - length[None, :, None] * image
        if turn + 1 < ITERS:
            scaled = residual / diagonal
            norm_next = norm_of(local_inner(residual, scaled))
            direction = scaled + (norm_next / norm_now)[None, :, None] * direction
            norm_now = norm_next
    return (dipoles, residual)


def solution(mesh):
    placed = (
        P(None, ("row", "col")),
        P(("row", "col")),
        P(),
        P(),
        P(),
        P(),
        P(None, None, ("row", "col")),
        P(None, None, ("row", "col")),
    )
    return jax.shard_map(
        shards,
        mesh=mesh,
        in_specs=placed,
        out_specs=(P(None, None, ("row", "col")), P(None, None, ("row", "col"))),
        check_vma=False,
    )
```

profile of v0, /device:TPU:1, one launch (start us, length us, event | category | flops | bytes accessed | tf_op | source)
XLA Modules:
  0.0 1113.5 jit_solution(6405055248834296242)
XLA Ops:
  7.2 0.8 fusion.123
  8.0 0.7 broadcast_multiply_fusion.4
  8.8 38.4 %all-gather = f32[32,32,4]{1,2,0:T(4,128)S(1)} all-gather(f32[1,32,4]{1,2,0:T(4,128)S(1)} %maximum_bitcast_fusion), channel_id=1, replica_groups=mesh['row'=32,'col'=16] {'row'}, dimensions={0}, use_global_device_ids=true | all-gather | bytes 16896 | tf_op jit(solution)/shard_map/all_gather | solution.py:63
  47.2 36.0 %all-gather.1 = f32[16,32,4]{1,2,0:T(4,128)S(1)} all-gather(f32[1,32,4]{1,2,0:T(4,128)S(1)} %maximum_bitcast_fusion), channel_id=1, replica_groups=mesh['row'=32,'col'=16] {'col'}, dimensions={0}, use_global_device_ids=true | all-gather | bytes 8704 | tf_op jit(solution)/shard_map/all_gather | solution.py:52
  83.3 36.2 %all-gather.2 = f32[32,32,24]{1,2,0:T(8,128)S(1)} all-gather(f32[1,32,24]{1,2,0:T(8,128)} %bitcast.285), channel_id=1, replica_groups=mesh['row'=32,'col'=16] {'row'}, dimensions={0}, use_global_device_ids=true | all-gather | bytes 101376 | tf_op jit(solution)/shard_map/all_gather | solution.py:64
  119.8 29.7 %while.52 = (s32[]{:T(128)}, f32[24,512]{1,0:T(8,128)S(1)}, s32[8]{0:T(128)S(1)}, f32[4,1024]{1,0:T(4,128)S(1)}, f32[4,512]{1,0:T(4,128)S(1)}, /*index=5*/s32[]{...) while((s32[]{:T(128)}, f32[24,512]{1,0:T(8,128)S(1)}, ...), condition=%wide.region_1.2_spmd.clone, body=%wide.region_0.1_spmd.clone.sunk | while | flops 61042200 | bytes 6166769 | solution.py:31
  119.8 0.7 dynamic_slice.119
  121.7 1.8 fusion.164
  123.5 0.7 dynamic_slice.119
  125.4 1.8 fusion.164
  129.1 1.8 fusion.164
  132.9 1.8 fusion.164
  136.6 1.8 fusion.164
  140.3 1.8 fusion.164
  144.0 1.8 fusion.164
  147.7 1.8 fusion.164
  149.5 0.8 copy.30
  150.5 62.0 %reduce-scatter.13.cloned.1.call-done = f32[32,24]{1,0:T(8,128)} async-done(((f32[512,24]{1,0:T(8,128)}), f32[32,24]{1,0:T(8,128)}) %reduce-scatter.13.cloned.1.call-update) | async-done | bytes 3088
  212.5 0.8 copy.31
  213.3 37.5 %all-gather.3 = f32[32,32,24]{1,2,0:T(8,128)S(1)} all-gather(f32[1,32,24]{1,2,0:T(8,128)S(1)} %get-tuple-element.620), channel_id=1, replica_groups=mesh['row'=32,'col'=16] {'row'}, dimensions={0}, use_global_device_ids=true | all-gather | bytes 101376 | tf_op jit(solution)/shard_map/all_gather | solution.py:64
  251.0 29.7 %while.53 = (s32[]{:T(128)}, f32[24,512]{1,0:T(8,128)S(1)}, s32[8]{0:T(128)S(1)}, f32[4,1024]{1,0:T(4,128)S(1)}, f32[4,512]{1,0:T(4,128)S(1)}, /*index=5*/s32[]{...) while((s32[]{:T(128)}, f32[24,512]{1,0:T(8,128)S(1)}, ...), condition=%wide.region_6.7_spmd.clone, body=%wide.region_5.6_spmd.clone.sunk | while | flops 61042200 | bytes 6166769 | solution.py:31
  252.9 1.8 fusion.169
  256.7 1.8 fusion.169
  260.4 1.8 fusion.169
  264.1 1.8 fusion.169
  267.8 1.8 fusion.169
  271.5 1.8 fusion.169
  275.2 1.8 fusion.169
  278.9 1.8 fusion.169
  280.7 0.8 copy.32
  281.7 67.1 %reduce-scatter.15.cloned.1.call-done = f32[32,24]{1,0:T(8,128)} async-done(((f32[512,24]{1,0:T(8,128)}), f32[32,24]{1,0:T(8,128)}) %reduce-scatter.15.cloned.1.call-update) | async-done | bytes 3088
  348.8 0.8 copy.33
  349.7 99.7 %all-reduce = (f32[8]{0:T(128)S(1)}, f32[8]{0:T(128)S(1)}) all-reduce(f32[8]{0:T(128)S(1)} %get-tuple-element.543, f32[8]{0:T(128)S(1)} %get-tuple-element.542), channel_id=1, replica_groups=mesh['row'=32,'col'=16] {'row','col'}, use_global_device_ids=true, to_apply=%region_4.5 | all-reduce | flops 16 | bytes 128 | tf_op jit(solution)/shard_map/psum | solution.py:91
  449.6 94.4 %psum.44 = f32[8]{0:T(128)S(1)} all-reduce(f32[8]{0:T(128)S(1)} %multiply_reduce_fusion.3), channel_id=1, replica_groups=mesh['row'=32,'col'=16] {'row','col'}, use_global_device_ids=true, to_apply=%region_11.12 | all-reduce | flops 8 | bytes 64 | tf_op jit(solution)/shard_map/psum | solution.py:91
  544.1 36.3 %all-gather.4 = f32[32,32,24]{1,2,0:T(8,128)S(1)} all-gather(f32[1,32,24]{1,2,0:T(8,128)S(1)} %fusion.139), channel_id=1, replica_groups=mesh['row'=32,'col'=16] {'row'}, dimensions={0}, use_global_device_ids=true | all-gather | bytes 101376 | tf_op jit(solution)/shard_map/all_gather | solution.py:64
  580.7 29.7 %while.54 = (s32[]{:T(128)}, f32[24,512]{1,0:T(8,128)S(1)}, s32[8]{0:T(128)S(1)}, f32[4,1024]{1,0:T(4,128)S(1)}, f32[4,512]{1,0:T(4,128)S(1)}, /*index=5*/s32[]{...) while((s32[]{:T(128)}, f32[24,512]{1,0:T(8,128)S(1)}, ...), condition=%wide.region_13.14_spmd.clone, body=%wide.region_12.13_spmd.clone.sunk | while | flops 61042200 | bytes 6166769 | solution.py:31
  582.6 1.8 fusion.174
  586.3 1.8 fusion.174
  590.0 1.8 fusion.174
  593.7 1.8 fusion.174
  597.4 1.8 fusion.174
  601.2 1.8 fusion.174
  604.9 1.8 fusion.174
  608.6 1.8 fusion.174
  610.4 0.8 copy.34
  611.3 65.6 %reduce-scatter.17.cloned.1.call-done = f32[32,24]{1,0:T(8,128)} async-done(((f32[512,24]{1,0:T(8,128)}), f32[32,24]{1,0:T(8,128)}) %reduce-scatter.17.cloned.1.call-update) | async-done | bytes 3088
  676.9 0.8 copy.35
  677.9 99.9 %psum.45 = f32[8]{0:T(128)S(1)} all-reduce(f32[8]{0:T(128)S(1)} %multiply_reduce_fusion.2), channel_id=1, replica_groups=mesh['row'=32,'col'=16] {'row','col'}, use_global_device_ids=true, to_apply=%region_16.17 | all-reduce | flops 8 | bytes 64 | tf_op jit(solution)/shard_map/psum | solution.py:98
  778.0 94.4 %psum.46 = f32[8]{0:T(128)S(1)} all-reduce(f32[8]{0:T(128)S(1)} %get-tuple-element.618), channel_id=1, replica_groups=mesh['row'=32,'col'=16] {'row','col'}, use_global_device_ids=true, to_apply=%region_18.19 | all-reduce | flops 8 | bytes 64 | tf_op jit(solution)/shard_map/psum | solution.py:91
  872.5 36.2 %all-gather.5 = f32[32,32,24]{1,2,0:T(8,128)S(1)} all-gather(f32[1,32,24]{1,2,0:T(8,128)S(1)} %fusion.132), channel_id=1, replica_groups=mesh['row'=32,'col'=16] {'row'}, dimensions={0}, use_global_device_ids=true | all-gather | bytes 101376 | tf_op jit(solution)/shard_map/all_gather | solution.py:64
  909.0 29.7 %while.55 = (s32[]{:T(128)}, f32[24,512]{1,0:T(8,128)S(1)}, s32[8]{0:T(128)S(1)}, f32[4,1024]{1,0:T(4,128)S(1)}, f32[4,512]{1,0:T(4,128)S(1)}, /*index=5*/s32[]{...) while((s32[]{:T(128)}, f32[24,512]{1,0:T(8,128)S(1)}, ...), condition=%wide.region_20.21_spmd.clone, body=%wide.region_19.20_spmd.clone.sunk | while | flops 61042200 | bytes 6166769 | solution.py:31
  910.9 1.8 fusion.179
  914.6 1.8 fusion.179
  918.3 1.8 fusion.179
  922.0 1.8 fusion.179
  925.7 1.8 fusion.179
  929.4 1.8 fusion.179
  933.1 1.8 fusion.179
  936.9 1.8 fusion.179
  938.7 0.8 copy.36
  939.5 66.0 %reduce-scatter.19.cloned.1.call-done = f32[32,24]{1,0:T(8,128)} async-done(((f32[512,24]{1,0:T(8,128)}), f32[32,24]{1,0:T(8,128)}) %reduce-scatter.19.cloned.1.call-update) | async-done | bytes 3088
  1005.5 0.8 copy.37
  1006.5 99.7 %psum.47 = f32[8]{0:T(128)S(1)} all-reduce(f32[8]{0:T(128)S(1)} %multiply_reduce_fusion), channel_id=1, replica_groups=mesh['row'=32,'col'=16] {'row','col'}, use_global_device_ids=true, to_apply=%region_23.24 | all-reduce | flops 8 | bytes 64 | tf_op jit(solution)/shard_map/psum | solution.py:98
  1106.3 0.7 multiply_subtract_fusion
  (400 shorter events, 37.5 us)
Async XLA Ops:
  7.2 205.3 %reduce-scatter.13.cloned.1.call-start = ((), (), s32[]{:S(2)}) async-start(), calls=%async_computation.4 | async-start | bytes 278528
  119.8 30.7 %copy-start.2 = (f32[8]{0:T(128)S(1)}, f32[8]{0:T(128)}, u32[]{:S(2)}) copy-start(f32[8]{0:T(128)} %param.21) | copy-start | bytes 100
  119.8 93.5 %copy-start = (f32[3,8,32]{2,1,0:T(8,128)S(1)}, f32[3,8,32]{2,1,0:T(8,128)}, u32[]{:S(2)}) copy-start(f32[3,8,32]{2,1,0:T(8,128)} %param.23) | copy-start | bytes 9220
  119.8 93.5 %copy-start.1 = (f32[3,8,32]{2,1,0:T(8,128)S(1)}, f32[3,8,32]{2,1,0:T(8,128)}, u32[]{:S(2)}) copy-start(f32[3,8,32]{2,1,0:T(8,128)} %param.22) | copy-start | bytes 9220
  150.4 198.4 %reduce-scatter.15.cloned.1.call-start = ((), (), s32[]{:S(2)}) async-start(), calls=%async_computation.5 | async-start | bytes 278528
  281.6 395.4 %reduce-scatter.17.cloned.1.call-start = ((), (), s32[]{:S(2)}) async-start(), calls=%async_computation.6 | async-start | bytes 278528
  611.2 394.3 %reduce-scatter.19.cloned.1.call-start = ((), (), s32[]{:S(2)}) async-start(), calls=%async_computation.7 | async-start | bytes 278528
Sparse Core Ops, SparseCore 0:
  150.5 61.9 reduce-scatter.12
  281.7 66.9 reduce-scatter.14
  611.4 65.5 reduce-scatter.16
  939.6 65.8 reduce-scatter.18
where the time goes:
time: 1120 us; the launch traced here: 1110 us
  blocking collectives  709 us (63%)
  waiting for transfers between devices  261 us (23%)
  matrix products  58.2 us (5%)
  local copies, waits for them, and re-layouts  29.6 us (3%)
  loops' own time  25.3 us (2%)
  other arithmetic  16.8 us (2%)
  between operations  13.9 us (1%)
    psum x3, blocking collectives, norm_of(): return lax.psum(values, ('row', 'col'))  289 us
    unnamed x8, waiting for transfers between devices  261 us
    psum x2, blocking collectives, shards(): length = norm_now / lax.psum(local_inner(direction, image), ('row', 'col'))  200 us
    all_gather x4, blocking collectives, couple(): column_vector = lax.all_gather(flat, 'row', axis=1, tiled=True)  146 us
    dot_general x32, matrix products, step(): added = jnp.einsum('bfj,abji->afi', vector_part, tensor, precision=PRECISE)  57.4 us
    all_gather x1, blocking collectives, couple(): column_sites = lax.all_gather(local_sites, 'row', axis=1, tiled=True)  38.4 us
    all_gather x1, blocking collectives, shards(): row_sites = lax.all_gather(local_sites, 'col', axis=1, tiled=True)  36 us
    another operation x4, loops' own time, over_columns(): return lax.scan(turn, carry, jnp.arange(width // 128, dtype=jnp.int32))[0]  25.3 us
  transfers between devices with their start and end apart: 4, of which 4 were waited for; matrix products, arithmetic and copies ran while one was open for 0% of the time, Pallas kernels for 0%

commit v1 on v0

v1 whole, which is shorter than its diff:
```python
import functools

import jax
import jax.numpy as jnp
from jax import lax
from jax.experimental import pallas as pl
from jax.experimental.pallas import tpu as pltpu
from jax.sharding import PartitionSpec as P

MESH = pl.DeviceIdType.MESH
F32, BF16 = jnp.float32, jnp.bfloat16
APPLICATIONS = 4
PAIRS = ((0, 0), (1, 1), (2, 2), (0, 1), (0, 2), (1, 2))
LANES = 128


def pick(indices, table, count):
    value = jnp.full(indices.shape, table[0], F32)
    for number in range(1, count):
        value = jnp.where(indices == number, table[number], value)
    return value


def kernel(
    rows, cols, piece, side,
    positions, types, alphas, omegas, radii, frequencies, field, start,
    dipoles_out, residual_out,
    gathered, partial, landed, sites, own_sites, coupling, tall, wide, sums,
    gather_send, gather_recv, sites_send, sites_recv, fold_send, fold_recv, sum_send, sum_recv,
):
    nfreq, ntypes = frequencies.shape[0], alphas.shape[0]
    row, col = lax.axis_index("row"), lax.axis_index("col")

    barrier = pltpu.get_barrier_semaphore()

    def greet_row(k, _):
        pl.semaphore_signal(barrier, inc=1, device_id=(lax.rem(row + k, rows), col), device_id_type=MESH)
        return 0

    def greet_col(k, _):
        pl.semaphore_signal(barrier, inc=1, device_id=(row, lax.rem(col + k, cols)), device_id_type=MESH)
        return 0

    lax.fori_loop(1, rows, greet_row, 0)
    lax.fori_loop(1, cols, greet_col, 0)

    def send_row(source, target, send_sem, recv_sem):
        def one(k, _):
            pltpu.make_async_remote_copy(
                src_ref=source, dst_ref=target, send_sem=send_sem, recv_sem=recv_sem,
                device_id=(lax.rem(row + k, rows), col), device_id_type=MESH,
            ).start()
            return 0

        lax.fori_loop(1, rows, one, 0)

    def send_col(source_of, target, send_sem, recv_sem):
        def one(k, _):
            peer = lax.rem(col + k, cols)
            pltpu.make_async_remote_copy(
                src_ref=source_of(peer), dst_ref=target, send_sem=send_sem, recv_sem=recv_sem,
                device_id=(row, peer), device_id_type=MESH,
            ).start()
            return 0

        lax.fori_loop(1, cols, one, 0)

    def wait_for(buffer, count, sem):
        view = buffer.at[pl.ds(0, count)]
        pltpu.make_async_copy(view, view, sem).wait()

    def packed(ref):
        return jnp.concatenate([ref[0], ref[1], ref[2]], axis=1)

    lane = lax.broadcasted_iota(jnp.int32, (nfreq, LANES), 1)
    used = lane < 3 * piece
    level = lax.broadcasted_iota(jnp.int32, (nfreq, LANES), 0)
    kinds = types[...]
    radius = pick(kinds, radii, ntypes)
    place = positions[...] * side
    pad = jnp.zeros((nfreq - 4, piece), F32)
    site = jnp.concatenate([place, radius, pad], axis=0)
    start_packed = packed(start)
    message = jnp.concatenate([start_packed, site], axis=1)
    kinds_packed = jnp.broadcast_to(jnp.concatenate([kinds] * (LANES // piece), axis=1), (nfreq, LANES))
    omega = pick(kinds_packed, omegas, ntypes)
    alpha = pick(kinds_packed, alphas, ntypes)
    ratio = pick(level, frequencies, nfreq) / omega
    diagonal = (1.0 + ratio * ratio) / alpha
    zeros_tail = jnp.zeros((nfreq, LANES - 3 * piece), F32)
    start_full = jnp.concatenate([start_packed, zeros_tail], axis=1)
    field_full = jnp.concatenate([packed(field), zeros_tail], axis=1)

    gathered[0, row] = message
    sites[col] = message
    pl.semaphore_wait(barrier, rows + cols - 2)
    send_row(gathered.at[0, row], gathered.at[0, row], gather_send.at[0], gather_recv.at[0])
    send_col(lambda peer: sites.at[col], sites.at[col], sites_send, sites_recv)

    wait_for(sites, cols - 1, sites_recv)
    for c in range(cols):
        own_sites[:, c * piece:(c + 1) * piece] = sites[c][:, 3 * piece:]
    wait_for(gathered.at[0], rows - 1, gather_recv.at[0])

    width = cols * piece

    def build(s, _):
        turned = gathered[0, s].T[3 * piece:, :]
        base = pl.multiple_of(s * piece, piece)
        column = [jnp.broadcast_to(turned[:, q:q + 1], (piece, LANES)) for q in range(4)]
        for n in range(width // LANES):
            span = slice(n * LANES, (n + 1) * LANES)
            offset = [column[q] - own_sites[q:q + 1, span] for q in range(3)]
            reach = column[3] + own_sites[3:4, span]
            square = offset[0] * offset[0] + offset[1] * offset[1] + offset[2] * offset[2] + reach * reach
            inverse = lax.rsqrt(square)
            second = inverse * inverse
            cube = second * inverse
            fifth = -3.0 * (cube * second)
            weighted = [offset[q] * fifth for q in range(3)]
            for number, (a, b) in enumerate(PAIRS):
                value = weighted[a] * offset[b]
                if a == b:
                    value = value + cube
                high = value.astype(BF16)
                coupling[number, 0, pl.ds(base, piece), span] = high
                coupling[number, 1, pl.ds(base, piece), span] = (value - high.astype(F32)).astype(BF16)
        return 0

    lax.fori_loop(0, rows, build, 0)

    base = pl.multiple_of(row * piece, piece)
    group = LANES // piece
    span = pl.ds(pl.multiple_of((col // group) * LANES, LANES), LANES)
    shift = lax.rem(col, group) * piece
    apart = (
        lax.broadcasted_iota(jnp.int32, (piece, LANES), 0) + shift
        != lax.broadcasted_iota(jnp.int32, (piece, LANES), 1)
    )
    for number in range(len(PAIRS)):
        for part in range(2):
            block = coupling[number, part, pl.ds(base, piece), span].astype(F32)
            coupling[number, part, pl.ds(base, piece), span] = jnp.where(apart, block, 0.0).astype(BF16)

    def apply(turn):
        for a in range(3):
            for t in range(rows * piece // LANES):
                tall[a, :, t * LANES:(t + 1) * LANES] = jnp.concatenate(
                    [gathered[turn, t * group + q][:, a * piece:(a + 1) * piece] for q in range(group)], axis=1
                )
        highs, lows = [], []
        for a in range(3):
            value = tall[a]
            high = value.astype(BF16).astype(F32)
            highs.append(high)
            lows.append(value - high)
        out = [jnp.zeros((nfreq, width), F32) for _ in range(3)]

        def dot(left, number, part):
            return jnp.dot(
                jnp.concatenate(left, axis=0).astype(BF16), coupling[number, part], preferred_element_type=F32
            )

        for number, (a, b) in enumerate(PAIRS):
            if a == b:
                main = dot([highs[a], lows[a]], number, 0)
                rest = dot([highs[a], lows[a]], number, 1)
                out[a] = out[a] + (main[:nfreq] + (main[nfreq:] + rest[:nfreq]))
            else:
                main = dot([highs[b], lows[b], highs[a], lows[a]], number, 0)
                rest = dot([highs[b], highs[a]], number, 1)
                out[a] = out[a] + (main[:nfreq] + (main[nfreq:2 * nfreq] + rest[:nfreq]))
                out[b] = out[b] + (main[2 * nfreq:3 * nfreq] + (main[3 * nfreq:] + rest[nfreq:]))
        for a in range(3):
            wide[a] = out[a]
        for c in range(cols):
            cut = slice(c * piece, (c + 1) * piece)
            partial[turn, c] = jnp.concatenate([wide[0, :, cut], wide[1, :, cut], wide[2, :, cut], zeros_tail], axis=1)
        landed[turn, col] = partial[turn, col]
        send_col(lambda peer: partial.at[turn, peer], landed.at[turn, col], fold_send.at[turn], fold_recv.at[turn])
        wait_for(landed.at[turn], cols - 1, fold_recv.at[turn])
        total = landed[turn, 0]
        for c in range(1, cols):
            total = total + landed[turn, c]
        return total

    def spread(turn, value):
        gathered[turn, row] = value
        send_row(gathered.at[turn, row], gathered.at[turn, row], gather_send.at[turn], gather_recv.at[turn])
        wait_for(gathered.at[turn], rows - 1, gather_recv.at[turn])

    powers = [field_full - diagonal * start_full - apply(0)]
    scaled = []
    for turn in range(1, APPLICATIONS):
        scaled.append(powers[-1] / diagonal)
        spread(turn, scaled[-1])
        powers.append(apply(turn))

    moments = jnp.zeros((nfreq, LANES), F32)
    for k, (i, j) in enumerate(((0, 0), (0, 1), (1, 1), (1, 2), (2, 2), (2, 3))):
        local = jnp.sum(jnp.where(used, scaled[i] * powers[j], 0.0), axis=1, keepdims=True)
        moments = jnp.where(lane == k, local, moments)
    sums[0, row] = moments
    send_row(sums.at[0, row], sums.at[0, row], sum_send.at[0], sum_recv.at[0])
    wait_for(sums.at[0], rows - 1, sum_recv.at[0])
    total = sums[0, 0]
    for r in range(1, rows):
        total = total + sums[0, r]
    sums[1, col] = total
    send_col(lambda peer: sums.at[1, col], sums.at[1, col], sum_send.at[1], sum_recv.at[1])
    wait_for(sums.at[1], cols - 1, sum_recv.at[1])
    total = sums[1, 0]
    for c in range(1, cols):
        total = total + sums[1, c]

    m = [jnp.broadcast_to(total[:, k:k + 1], (nfreq, LANES)) for k in range(6)]
    a0 = m[1] / m[0]
    h0 = m[0]
    h1 = m[2] - a0 * m[1]
    a1 = (m[3] - 2.0 * a0 * m[2] + a0 * a0 * m[1]) / h1
    b1 = h1 / h0
    c1 = -(a0 + a1)
    c0 = a0 * a1 - b1
    h2 = m[4] + c1 * m[3] + c0 * m[2]
    a2 = (m[5] + c1 * m[4] + c0 * m[3]) / h2 + c1
    b2 = h2 / h1
    e2 = c1 - a2
    e1 = c0 - a2 * c1 - b2
    e0 = b2 * a0 - a2 * c0
    top = 1.0 / (e2 - 1.0 - e1 + e0)
    p3, p2, p1, p0 = top, e2 * top, e1 * top, e0 * top
    s2 = -p3
    s1 = -p2 - s2
    s0 = -p1 - s1
    residual = p0 * powers[0] + p1 * powers[1] + p2 * powers[2] + p3 * powers[3]
    dipoles = start_full + (s0 * scaled[0] + s1 * scaled[1] + s2 * scaled[2])
    for a in range(3):
        dipoles_out[a] = dipoles[:, a * piece:(a + 1) * piece]
        residual_out[a] = residual[:, a * piece:(a + 1) * piece]

    for turn in range(APPLICATIONS):
        wait_for(gathered.at[turn], rows - 1, gather_send.at[turn])
        wait_for(landed.at[turn], cols - 1, fold_send.at[turn])
    wait_for(sites, cols - 1, sites_send)
    wait_for(sums.at[0], rows - 1, sum_send.at[0])
    wait_for(sums.at[1], cols - 1, sum_send.at[1])


def solution(mesh):
    rows, cols = mesh.shape["row"], mesh.shape["col"]

    def shards(positions, atom_types, alpha_table, omega_table, radius_table, frequencies, field, start_dipoles):
        piece, nfreq = positions.shape[1], frequencies.shape[0]
        side = (10.0 * piece * rows * cols) ** (1.0 / 3.0)
        vmem = pl.BlockSpec(memory_space=pltpu.VMEM)
        smem = pl.BlockSpec(memory_space=pltpu.SMEM)
        tile = (nfreq, LANES)
        dma = pltpu.SemaphoreType.DMA
        return pl.pallas_call(
            functools.partial(kernel, rows, cols, piece, side),
            out_shape=(jax.ShapeDtypeStruct(field.shape, F32),) * 2,
            in_specs=[vmem, vmem, smem, smem, smem, smem, vmem, vmem],
            out_specs=(vmem, vmem),
            scratch_shapes=[
                pltpu.VMEM((APPLICATIONS, rows) + tile, F32),
                pltpu.VMEM((APPLICATIONS, cols) + tile, F32),
                pltpu.VMEM((APPLICATIONS, cols) + tile, F32),
                pltpu.VMEM((cols,) + tile, F32),
                pltpu.VMEM((nfreq, cols * piece), F32),
                pltpu.VMEM((len(PAIRS), 2, rows * piece, cols * piece), BF16),
                pltpu.VMEM((3, nfreq, rows * piece), F32),
                pltpu.VMEM((3, nfreq, cols * piece), F32),
                pltpu.VMEM((2, rows) + tile, F32),
                dma((APPLICATIONS,)), dma((APPLICATIONS,)),
                dma, dma,
                dma((APPLICATIONS,)), dma((APPLICATIONS,)),
                dma((2,)), dma((2,)),
            ],
            compiler_params=pltpu.CompilerParams(
                collective_id=0, has_side_effects=True, vmem_limit_bytes=48 * 1024 * 1024
            ),
        )(
            positions, atom_types.reshape(1, piece), alpha_table, omega_table, radius_table, frequencies,
            field, start_dipoles,
        )

    placed = (
        P(None, ("row", "col")),
        P(("row", "col")),
        P(),
        P(),
        P(),
        P(),
        P(None, None, ("row", "col")),
        P(None, None, ("row", "col")),
    )
    return jax.shard_map(
        shards,
        mesh=mesh,
        in_specs=placed,
        out_specs=(P(None, None, ("row", "col")), P(None, None, ("row", "col"))),
        check_vma=False,
    )
```

time: 1120 us -> 105 us (0.09)
  blocking collectives: 709 us -> 0 us
  waiting for transfers between devices: 261 us -> 0 us
  Pallas kernels: 0 us -> 98.4 us
  matrix products: 58.2 us -> 0 us
  loops' own time: 25.3 us -> 0 us
  local copies, waits for them, and re-layouts: 29.6 us -> 5.27 us
  other arithmetic: 16.8 us -> 0 us
  between operations: 13.9 us -> 0.67 us
    psum x5 -> x0, blocking collectives: 488 us -> none  [the longest x3 289 us: norm_of(): return lax.psum(values, ('row', 'col'))]
    unnamed x8 -> x0, waiting for transfers between devices: 261 us -> none
    all_gather x6 -> x0, blocking collectives: 220 us -> none  [the longest x4 146 us: couple(): column_vector = lax.all_gather(flat, 'row', axis=1, tiled=True)]
    pallas_call x0 -> x1, Pallas kernels: none -> 98.4 us  [shards(): pl.pallas_call(functools.partial(kernel, rows, cols, piece, side), out_sh...]
    dot_general x33 -> x0, matrix products: 58.2 us -> none  [the longest x32 57.4 us: step(): added = jnp.einsum('bfj,abji->afi', vector_part, tensor, precision=PRECISE)]
    another operation x4 -> x0, loops' own time: 25.3 us -> none  [over_columns(): return lax.scan(turn, carry, jnp.arange(width // 128, dtype=jnp.int32))[0]]
    dynamic_slice x64 -> x0, local copies, waits for them, and re-layouts: 21.6 us -> none  [the longest x32 21.3 us: over_columns(): return lax.scan(turn, carry, jnp.arange(width // 128, dtype=jnp.int32))[0]]
    mul x97 -> x0, other arithmetic: 11.5 us -> none  [the longest x32 5.37 us: tensor_block(): dyadic = -3.0 * offsets[:, None] * offsets[None, :] * inverse_fifth]
  transfers between devices with their start and end apart: 4 -> 0, of which waited for: 4 -> 0; matrix products, arithmetic and copies ran while one was open for 0% -> 0% of each run, Pallas kernels for 0% -> 0%
where the time goes in v1:
time: 105 us; the launch traced here: 104 us
  Pallas kernels  98.4 us (94%)
  local copies, waits for them, and re-layouts  5.27 us (5%)
    pallas_call x1, Pallas kernels, shards(): pl.pallas_call(functools.partial(kernel, rows, cols, piece, side), out_sh...  98.4 us
    unnamed x18, local copies, waits for them, and re-layouts  5.27 us

profile of v1, /device:TPU:1, one launch (start us, length us, event | category | flops | bytes accessed | tf_op | source)
XLA Modules:
  0.0 104.3 jit_solution(6718747329220137909)
XLA Ops:
  0.6 0.0 copy-start.5
  0.6 0.0 copy-start.4
  0.7 0.0 copy-start.3
  0.7 0.6 copy-done.5
  1.3 0.0 copy-done.4
  1.3 0.0 copy-done.3
  1.3 0.0 copy-start
  1.3 0.7 copy-done
  2.0 0.0 copy-start.1
  2.0 0.7 copy-done.1
  2.7 0.0 copy-start.2
  2.7 0.7 copy-done.2
  3.4 0.0 copy-start.6
  3.4 0.7 copy-done.6
  4.1 0.0 copy-start.7
  4.1 0.7 copy-done.7
  4.7 98.4 %shard_map.95 = (f32[3,8,32]{2,1,0:T(8,128)S(1)}, f32[3,8,32]{2,1,0:T(8,128)S(1)}) custom-call(f32[3,32]{1,0:T(4,128)S(1)} %copy-done.2, s32[1,32]{1,0:T(1,128)S(1)} %bitcast.1, f32[5]{0:T(128)S(1)} %copy-done.4, f32[5]{0:T(128)S(1)} %copy-done.5, f32[5]{0:T(128)S(1)} %copy-done.6, f32[8]{0:T(128)S(1)} %copy-done.7, f32[3,8,32]{2,1,0:T(8,128)S(1)} %copy-done, ...), custom_call_target="tpu_custom_call" | custom-call | tf_op jit(solution)/shard_map/pallas_call | solution.py:259
  103.1 0.6 copy.12
  103.7 0.6 copy.13
Async XLA Ops:
  0.6 0.7 copy-start.5
  0.6 0.7 copy-start.4
  0.7 0.7 copy-start.3
  1.3 0.7 copy-start
  2.0 0.7 copy-start.1
  2.7 0.7 copy-start.2
  3.4 0.7 copy-start.6
  4.1 0.7 copy-start.7

commit v2 on v1

v2 whole, which is shorter than its diff:
```python
import functools

import jax
import jax.numpy as jnp
from jax import lax
from jax.experimental import pallas as pl
from jax.experimental.pallas import tpu as pltpu
from jax.sharding import PartitionSpec as P

MESH = pl.DeviceIdType.MESH
F32, BF16 = jnp.float32, jnp.bfloat16
APPLICATIONS = 4
PAIRS = ((0, 0), (1, 1), (2, 2), (0, 1), (0, 2), (1, 2))
LANES = 128
TILE = 8
TILE_ORDER = (0, 1, 2, 3)
ROW_MINOR = 4
COL_MINOR = 2
MOMENTS = ((0, 0), (0, 1), (1, 1), (1, 2), (2, 2))


def pick(indices, table, count):
    value = jnp.full(indices.shape, table[0], F32)
    for number in range(1, count):
        value = jnp.where(indices == number, table[number], value)
    return value


def hops(step, length):
    return min(step, length - step)


def nearest_first(count, minor, hop_minor):
    major = count // minor
    offsets = [(far, near) for far in range(major) for near in range(minor)]
    return sorted(offsets, key=lambda o: (hops(o[0], major) + hop_minor * hops(o[1], minor), o))


def turned(me, count, minor):
    major = count // minor
    high, low = lax.div(me, minor), lax.rem(me, minor)
    highs = [lax.rem(high + step, major) * minor for step in range(major)]
    lows = [lax.rem(low + step, minor) for step in range(minor)]
    return highs, lows


def kernel(
    rows, cols, piece, side,
    positions_hbm, types_hbm, alphas_hbm, omegas_hbm, radii_hbm, frequencies_hbm, field_hbm, start_hbm,
    dipoles_out, residual_out,
    positions, types, alphas, omegas, radii, frequencies, field, start,
    gathered, partial, landed, sites, mates, own_sites, coupling, sums,
    load_sem, gather_send, gather_recv, sites_send, sites_recv, fold_send, fold_recv,
    mates_send, mates_recv, sum_send, sum_recv,
):
    nfreq, ntypes = frequencies.shape[0], alphas.shape[0]
    row, col = lax.axis_index("row"), lax.axis_index("col")
    tiles = rows // TILE
    group = LANES // piece
    width = cols * piece
    depth = TILE * piece

    loads = [
        pltpu.make_async_copy(source, target, load_sem.at[number])
        for number, (source, target) in enumerate((
            (positions_hbm, positions), (types_hbm, types), (alphas_hbm, alphas), (omegas_hbm, omegas),
            (radii_hbm, radii), (frequencies_hbm, frequencies), (field_hbm, field), (start_hbm, start),
        ))
    ]
    for load in loads:
        load.start()

    barrier = pltpu.get_barrier_semaphore()

    row_offsets = nearest_first(rows, ROW_MINOR, 1)
    col_offsets = nearest_first(cols, COL_MINOR, 0.5)
    row_high, row_low = turned(row, rows, ROW_MINOR)
    col_high, col_low = turned(col, cols, COL_MINOR)

    def row_peer(slot, sign):
        far, near = row_offsets[slot]
        return (row_high[sign * far % len(row_high)] + row_low[sign * near % len(row_low)], col)

    def col_peer(slot, sign):
        far, near = col_offsets[slot]
        return (row, col_high[sign * far % len(col_high)] + col_low[sign * near % len(col_low)])

    row_order = range(rows - 1, 0, -1)
    col_order = range(cols - 1, 0, -1)

    with jax.named_scope("greet"):
        for slot in row_order:
            pl.semaphore_signal(barrier, inc=1, device_id=row_peer(slot, 1), device_id_type=MESH)
        for slot in col_order:
            pl.semaphore_signal(barrier, inc=1, device_id=col_peer(slot, 1), device_id_type=MESH)

    def send_row(source, target, send_sem, recv_sem_of):
        for slot in row_order:
            pltpu.make_async_remote_copy(
                src_ref=source, dst_ref=target.at[slot], send_sem=send_sem, recv_sem=recv_sem_of(slot),
                device_id=row_peer(slot, -1), device_id_type=MESH,
            ).start()

    def send_col(source_of, target, send_sem, recv_sem, sign):
        for slot in col_order:
            pltpu.make_async_remote_copy(
                src_ref=source_of(slot), dst_ref=target.at[slot], send_sem=send_sem, recv_sem=recv_sem,
                device_id=col_peer(slot, sign), device_id_type=MESH,
            ).start()

    def wait_for(buffer, count, sem):
        view = buffer.at[pl.ds(0, count)]
        pltpu.make_async_copy(view, view, sem).wait()

    def packed(ref):
        return jnp.concatenate([ref[0], ref[1], ref[2]], axis=1)

    with jax.named_scope("load"):
        for load in loads:
            load.wait()
    lane = lax.broadcasted_iota(jnp.int32, (nfreq, LANES), 1)
    level = lax.broadcasted_iota(jnp.int32, (nfreq, LANES), 0)
    kinds = types[...]
    radius = pick(kinds, radii, ntypes)
    place = positions[...] * side
    pad = jnp.zeros((nfreq - 4, piece), F32)
    site = jnp.concatenate([place, radius, pad], axis=0)
    start_packed = packed(start)
    message = jnp.concatenate([start_packed, site], axis=1)
    gathered[0, 0] = message
    sites[0] = message
    with jax.named_scope("barrier"):
        pl.semaphore_wait(barrier, rows + cols - 2)
    with jax.named_scope("first send"):
        send_col(lambda slot: sites.at[0], sites, sites_send, sites_recv, -1)
        send_row(gathered.at[0, 0], gathered.at[0], gather_send.at[0], lambda slot: gather_recv.at[0, slot // TILE])

    kinds_packed = jnp.broadcast_to(jnp.concatenate([kinds] * group, axis=1), (nfreq, LANES))
    omega = pick(kinds_packed, omegas, ntypes)
    alpha = pick(kinds_packed, alphas, ntypes)
    ratio = pick(level, frequencies, nfreq) / omega
    diagonal = (1.0 + ratio * ratio) / alpha
    inverse_diagonal = alpha / (1.0 + ratio * ratio)
    zeros_tail = jnp.zeros((nfreq, LANES - 3 * piece), F32)
    start_full = jnp.concatenate([start_packed, zeros_tail], axis=1)
    field_full = jnp.concatenate([packed(field), zeros_tail], axis=1)
    source_full = field_full - diagonal * start_full

    with jax.named_scope("sites wait"):
        wait_for(sites, cols - 1, sites_recv)
    for c in range(cols):
        own_sites[:, c * piece:(c + 1) * piece] = sites[c][:, 3 * piece:]

    def build(tile, s, _):
        turned = gathered[0, tile * TILE + s].T[3 * piece:, :]
        base = pl.multiple_of(s * piece, piece)
        column = [jnp.broadcast_to(turned[:, q:q + 1], (piece, LANES)) for q in range(4)]
        for n in range(width // LANES):
            span = slice(n * LANES, (n + 1) * LANES)
            offset = [column[q] - own_sites[q:q + 1, span] for q in range(3)]
            reach = column[3] + own_sites[3:4, span]
            square = offset[0] * offset[0] + offset[1] * offset[1] + offset[2] * offset[2] + reach * reach
            inverse = lax.rsqrt(square)
            second = inverse * inverse
            cube = second * inverse
            fifth = -3.0 * (cube * second)
            weighted = [offset[q] * fifth for q in range(3)]
            for number, (a, b) in enumerate(PAIRS):
                value = weighted[a] * offset[b]
                if a == b:
                    value = value + cube
                high = value.astype(BF16)
                coupling[tile, number, 0, pl.ds(base, piece), span] = high
                coupling[tile, number, 1, pl.ds(base, piece), span] = (value - high.astype(F32)).astype(BF16)
        return 0

    def drop_self():
        apart = (
            lax.broadcasted_iota(jnp.int32, (piece, LANES), 0) != lax.broadcasted_iota(jnp.int32, (piece, LANES), 1)
        )
        for number in range(len(PAIRS)):
            for part in range(2):
                block = coupling[0, number, part, :piece, :LANES].astype(F32)
                coupling[0, number, part, :piece, :LANES] = jnp.where(apart, block, 0.0).astype(BF16)

    def unpack(block_of, count):
        blocks = [block_of(s) for s in range(count)]
        return [
            jnp.concatenate(
                [
                    jnp.concatenate([blocks[t + q][:, a * piece:(a + 1) * piece] for q in range(group)], axis=1)
                    for t in range(0, count, group)
                ],
                axis=1,
            )
            for a in range(3)
        ]

    def apply(turn):
        main = [None] * len(PAIRS)
        rest = [None] * len(PAIRS)
        for place, tile in enumerate(TILE_ORDER):
            with jax.named_scope(f"tile {tile} wait"):
                wait_for(gathered.at[turn], TILE - 1 if tile == 0 else TILE, gather_recv.at[turn, tile])
            if turn == 0:
                with jax.named_scope("build"):
                    lax.fori_loop(0, TILE, functools.partial(build, tile), 0)
                if tile == 0:
                    drop_self()
            with jax.named_scope("matmul"):
                values = unpack(lambda s: gathered[turn, tile * TILE + s], TILE)
                highs = [value.astype(BF16).astype(F32) for value in values]
                lows = [value - high for value, high in zip(values, highs)]

                def dot(left, number, part):
                    return jnp.dot(
                        jnp.concatenate(left, axis=0).astype(BF16), coupling[tile, number, part],
                        preferred_element_type=F32,
                    )

                for number, (a, b) in enumerate(PAIRS):
                    if a == b:
                        first = dot([highs[a], lows[a]], number, 0)
                        second = dot([highs[a], lows[a]], number, 1)
                    else:
                        first = dot([highs[b], lows[b], highs[a], lows[a]], number, 0)
                        second = dot([highs[b], highs[a]], number, 1)
                    main[number] = first if place == 0 else main[number] + first
                    rest[number] = second if place == 0 else rest[number] + second
        out = [None] * 3

        def add(a, value):
            out[a] = value if out[a] is None else out[a] + value

        for number, (a, b) in enumerate(PAIRS):
            add(a, main[number][:nfreq] + (main[number][nfreq:2 * nfreq] + rest[number][:nfreq]))
            if a != b:
                add(b, main[number][2 * nfreq:3 * nfreq] + (main[number][3 * nfreq:] + rest[number][nfreq:]))
        return out

    def fold(turn, out, tail):
        for c in range(cols):
            cut = slice(c * piece, (c + 1) * piece)
            block = jnp.concatenate([out[0][:, cut], out[1][:, cut], out[2][:, cut], tail], axis=1)
            if c == 0:
                landed[turn, 0] = block
            else:
                partial[turn, c] = block
        with jax.named_scope("fold send"):
            send_col(lambda slot: partial.at[turn, slot], landed.at[turn], fold_send.at[turn], fold_recv.at[turn], 1)
        with jax.named_scope("fold wait"):
            wait_for(landed.at[turn], cols - 1, fold_recv.at[turn])
        total = landed[turn, 0]
        for c in range(1, cols):
            total = total + landed[turn, c]
        return total

    def spread(turn, value):
        gathered[turn, 0] = value
        with jax.named_scope("gather send"):
            send_row(
                gathered.at[turn, 0], gathered.at[turn], gather_send.at[turn],
                lambda slot: gather_recv.at[turn, slot // TILE],
            )

    powers = [source_full - fold(0, apply(0), zeros_tail)]
    scaled = []
    for turn in range(1, APPLICATIONS):
        scaled.append(powers[-1] * inverse_diagonal)
        spread(turn, scaled[-1])
        if turn + 1 < APPLICATIONS:
            powers.append(fold(turn, apply(turn), zeros_tail))

    last = APPLICATIONS - 1
    mates[0] = scaled[last - 1]
    send_col(lambda slot: mates.at[0], mates, mates_send, mates_recv, -1)
    moments = zeros_tail
    tail_lane = lax.broadcasted_iota(jnp.int32, zeros_tail.shape, 1)
    for k, (i, j) in enumerate(MOMENTS):
        local = jnp.sum(scaled[i] * powers[j], axis=1, keepdims=True)
        moments = jnp.where(tail_lane == k, local, moments)
    out = apply(last)
    wait_for(mates, cols - 1, mates_recv)
    own = unpack(lambda s: mates[s], cols)
    local = jnp.sum(own[0] * out[0] + own[1] * out[1] + own[2] * out[2], axis=1, keepdims=True)
    moments = jnp.where(tail_lane == len(MOMENTS), local, moments)
    folded = fold(last, out, moments)
    sums[0] = folded
    with jax.named_scope("sum"):
        send_row(sums.at[0], sums, sum_send, lambda slot: sum_recv)
        powers.append(jnp.where(lane < 3 * piece, folded, 0.0))
        wait_for(sums, rows - 1, sum_recv)
    total = sums[0]
    for r in range(1, rows):
        total = total + sums[r]

    m = [jnp.broadcast_to(total[:, 3 * piece + k:3 * piece + k + 1], (nfreq, LANES)) for k in range(6)]
    a0 = m[1] / m[0]
    h0 = m[0]
    h1 = m[2] - a0 * m[1]
    a1 = (m[3] - 2.0 * a0 * m[2] + a0 * a0 * m[1]) / h1
    b1 = h1 / h0
    c1 = -(a0 + a1)
    c0 = a0 * a1 - b1
    h2 = m[4] + c1 * m[3] + c0 * m[2]
    a2 = (m[5] + c1 * m[4] + c0 * m[3]) / h2 + c1
    b2 = h2 / h1
    e2 = c1 - a2
    e1 = c0 - a2 * c1 - b2
    e0 = b2 * a0 - a2 * c0
    top = 1.0 / (e2 - 1.0 - e1 + e0)
    p3, p2, p1, p0 = top, e2 * top, e1 * top, e0 * top
    s2 = -p3
    s1 = -p2 - s2
    s0 = -p1 - s1
    residual = p0 * powers[0] + p1 * powers[1] + p2 * powers[2] + p3 * powers[3]
    dipoles = start_full + (s0 * scaled[0] + s1 * scaled[1] + s2 * scaled[2])
    for a in range(3):
        dipoles_out[a] = dipoles[:, a * piece:(a + 1) * piece]
        residual_out[a] = residual[:, a * piece:(a + 1) * piece]

    for turn in range(APPLICATIONS):
        wait_for(gathered.at[turn], rows - 1, gather_send.at[turn])
        wait_for(landed.at[turn], cols - 1, fold_send.at[turn])
    wait_for(sites, cols - 1, sites_send)
    wait_for(mates, cols - 1, mates_send)
    wait_for(sums, rows - 1, sum_send)


def solution(mesh):
    rows, cols = mesh.shape["row"], mesh.shape["col"]

    def shards(positions, atom_types, alpha_table, omega_table, radius_table, frequencies, field, start_dipoles):
        piece, nfreq = positions.shape[1], frequencies.shape[0]
        side = (10.0 * piece * rows * cols) ** (1.0 / 3.0)
        operands = (
            positions, atom_types.reshape(1, piece), alpha_table, omega_table, radius_table, frequencies,
            field, start_dipoles,
        )
        vmem = pl.BlockSpec(memory_space=pltpu.VMEM)
        tile = (nfreq, LANES)
        dma = pltpu.SemaphoreType.DMA
        places = [pltpu.VMEM] * 2 + [pltpu.SMEM] * 4 + [pltpu.VMEM] * 2
        return pl.pallas_call(
            functools.partial(kernel, rows, cols, piece, side),
            out_shape=(jax.ShapeDtypeStruct(field.shape, F32),) * 2,
            in_specs=[pl.BlockSpec(memory_space=pltpu.HBM)] * len(operands),
            out_specs=(vmem, vmem),
            scratch_shapes=[space(array.shape, array.dtype) for space, array in zip(places, operands)] + [
                pltpu.VMEM((APPLICATIONS, rows) + tile, F32),
                pltpu.VMEM((APPLICATIONS, cols) + tile, F32),
                pltpu.VMEM((APPLICATIONS, cols) + tile, F32),
                pltpu.VMEM((cols,) + tile, F32),
                pltpu.VMEM((cols,) + tile, F32),
                pltpu.VMEM((nfreq, cols * piece), F32),
                pltpu.VMEM((rows // TILE, len(PAIRS), 2, TILE * piece, cols * piece), BF16),
                pltpu.VMEM((rows,) + tile, F32),
                dma((len(operands),)),
                dma((APPLICATIONS,)), dma((APPLICATIONS, rows // TILE)),
                dma, dma,
                dma((APPLICATIONS,)), dma((APPLICATIONS,)),
                dma, dma,
                dma, dma,
            ],
            compiler_params=pltpu.CompilerParams(
                collective_id=0, has_side_effects=True, vmem_limit_bytes=64 * 1024 * 1024
            ),
        )(*operands)

    placed = (
        P(None, ("row", "col")),
        P(("row", "col")),
        P(),
        P(),
        P(),
        P(),
        P(None, None, ("row", "col")),
        P(None, None, ("row", "col")),
    )
    return jax.shard_map(
        shards,
        mesh=mesh,
        in_specs=placed,
        out_specs=(P(None, None, ("row", "col")), P(None, None, ("row", "col"))),
        check_vma=False,
    )
```

time: 105 us -> 85.5 us (0.81)
  Pallas kernels: 98.4 us -> 82.7 us
  local copies, waits for them, and re-layouts: 5.27 us -> 1.92 us
    pallas_call x1, Pallas kernels: 98.4 us -> 82.7 us  [shards(): pl.pallas_call(functools.partial(kernel, rows, cols, piece, side), out_sh...]
    unnamed x18 -> x4, local copies, waits for them, and re-layouts: 5.27 us -> 1.92 us
where the time goes in v2:
time: 85.5 us; the launch traced here: 85.3 us
  Pallas kernels  82.7 us (97%)
  local copies, waits for them, and re-layouts  1.92 us (2%)
    pallas_call x1, Pallas kernels, shards(): pl.pallas_call(functools.partial(kernel, rows, cols, piece, side), out_sh...  82.7 us
    unnamed x4, local copies, waits for them, and re-layouts  1.92 us

profile of v2, /device:TPU:1, one launch (start us, length us, event | category | flops | bytes accessed | tf_op | source)
XLA Modules:
  0.0 85.3 jit_solution(8008749655826422159)
XLA Ops:
  0.6 82.7 %shard_map.95 = (f32[3,8,32]{2,1,0:T(8,128)}, f32[3,8,32]{2,1,0:T(8,128)}) custom-call(f32[3,32]{1,0:T(4,128)} %positions_hbm.1, s32[1,32]{1,0:T(1,128)} %bitcast.1, f32[5]{0:T(128)} %alphas_hbm.1, f32[5]{0:T(128)} %omegas_hbm.1, f32[5]{0:T(128)} %radii_hbm.1, f32[8]{0:T(128)} %frequencies_hbm.1, f32[3,8,32]{2,1,0:T(8,128)} %field_hbm.1, f32[3,8,32]{2,1,0:T(8,128)} %start_hbm.1), custom_call_target="tpu_custom_call" | custom-call | tf_op jit(solution)/shard_map/pallas_call | solution.py:344
  83.3 0.0 copy-start
  83.4 1.3 %copy.12 = f32[3,8,32]{2,1,0:T(8,128)} copy(f32[3,8,32]{2,1,0:T(8,128)} %get-tuple-element.4) | data formatting | bytes 6144
  84.7 0.0 copy-done
  84.7 0.6 copy.13
Async XLA Ops:
  83.3 1.3 %copy-start = (f32[3,8,32]{2,1,0:T(8,128)S(1)}, f32[3,8,32]{2,1,0:T(8,128)}, u32[]{:S(2)}) copy-start(f32[3,8,32]{2,1,0:T(8,128)} %get-tuple-element.5) | copy-start | bytes 9220

commit v3 on v2

v3 whole, which is shorter than its diff:
```python
import functools

import jax
import jax.numpy as jnp
from jax import lax
from jax.experimental import pallas as pl
from jax.experimental.pallas import tpu as pltpu
from jax.sharding import PartitionSpec as P

MESH = pl.DeviceIdType.MESH
F32, BF16 = jnp.float32, jnp.bfloat16
APPLICATIONS = 4
PAIRS = ((0, 0), (1, 1), (2, 2), (0, 1), (0, 2), (1, 2))
LANES = 128
TILE = 8
ROW_MINOR = 4
COL_MINOR = 2
MOMENTS = ((0, 0), (0, 1), (1, 1), (1, 2), (2, 2))


def pick(indices, table, count):
    value = jnp.full(indices.shape, table[0], F32)
    for number in range(1, count):
        value = jnp.where(indices == number, table[number], value)
    return value


def hops(step, length):
    return min(step, length - step)


def nearest_first(count, minor, hop_minor):
    major = count // minor
    offsets = [(far, near) for far in range(major) for near in range(minor)]
    return sorted(offsets, key=lambda o: (hops(o[0], major) + hop_minor * hops(o[1], minor), o))


def turned(me, count, minor):
    major = count // minor
    high, low = lax.div(me, minor), lax.rem(me, minor)
    highs = [lax.rem(high + step, major) * minor for step in range(major)]
    lows = [lax.rem(low + step, minor) for step in range(minor)]
    return highs, lows


def kernel(
    rows, cols, piece, side,
    positions_hbm, types_hbm, alphas_hbm, omegas_hbm, radii_hbm, frequencies_hbm, field_hbm, start_hbm,
    dipoles_out, residual_out,
    positions, types, alphas, omegas, radii, frequencies, field, start,
    gathered, partial, landed, sites, mates, own_sites, columns, coupling, col_sums, row_sums,
    load_sem, gather_send, gather_recv, sites_send, sites_recv, fold_send, fold_recv,
    mates_send, mates_recv, sum_send, sum_recv,
):
    nfreq, ntypes = frequencies.shape[0], alphas.shape[0]
    row, col = lax.axis_index("row"), lax.axis_index("col")
    tiles = rows // TILE
    group = LANES // piece
    depth = TILE * piece

    loads = [
        pltpu.make_async_copy(source, target, load_sem.at[number])
        for number, (source, target) in enumerate((
            (positions_hbm, positions), (types_hbm, types), (alphas_hbm, alphas), (omegas_hbm, omegas),
            (radii_hbm, radii), (frequencies_hbm, frequencies), (field_hbm, field), (start_hbm, start),
        ))
    ]
    barrier = pltpu.get_barrier_semaphore()

    row_offsets = nearest_first(rows, ROW_MINOR, 1)
    col_offsets = nearest_first(cols, COL_MINOR, 0.5)
    row_high, row_low = turned(row, rows, ROW_MINOR)
    col_high, col_low = turned(col, cols, COL_MINOR)

    def row_peer(slot, sign):
        far, near = row_offsets[slot]
        return (row_high[sign * far % len(row_high)] + row_low[sign * near % len(row_low)], col)

    def col_peer(slot, sign):
        far, near = col_offsets[slot]
        return (row, col_high[sign * far % len(col_high)] + col_low[sign * near % len(col_low)])

    row_order = range(rows - 1, 0, -1)
    col_order = range(cols - 1, 0, -1)

    with jax.named_scope("greet"):
        for slot in row_order:
            pl.semaphore_signal(barrier, inc=1, device_id=row_peer(slot, 1), device_id_type=MESH)
        for slot in col_order:
            pl.semaphore_signal(barrier, inc=1, device_id=col_peer(slot, 1), device_id_type=MESH)

    for load in loads:
        load.start()

    def send_row(source_of, target, send_sem, recv_sem, sign, slots=row_order):
        for slot in slots:
            pltpu.make_async_remote_copy(
                src_ref=source_of(slot), dst_ref=target.at[slot], send_sem=send_sem, recv_sem=recv_sem,
                device_id=row_peer(slot, sign), device_id_type=MESH,
            ).start()

    def send_col(source, target, send_sem, recv_sem):
        for slot in col_order:
            pltpu.make_async_remote_copy(
                src_ref=source, dst_ref=target.at[slot], send_sem=send_sem, recv_sem=recv_sem,
                device_id=col_peer(slot, -1), device_id_type=MESH,
            ).start()

    def wait_for(buffer, count, sem):
        view = buffer.at[pl.ds(0, count)]
        pltpu.make_async_copy(view, view, sem).wait()

    def packed(ref):
        return jnp.concatenate([ref[0], ref[1], ref[2]], axis=1)

    with jax.named_scope("load"):
        for load in loads:
            load.wait()
    lane = lax.broadcasted_iota(jnp.int32, (nfreq, LANES), 1)
    level = lax.broadcasted_iota(jnp.int32, (nfreq, LANES), 0)
    kinds = types[...]
    radius = pick(kinds, radii, ntypes)
    place = positions[...] * side
    pad = jnp.zeros((nfreq - 4, piece), F32)
    site = jnp.concatenate([place, radius, pad], axis=0)
    start_packed = packed(start)
    message = jnp.concatenate([start_packed, site], axis=1)
    gathered[0, 0] = message
    sites[0] = message
    with jax.named_scope("barrier"):
        pl.semaphore_wait(barrier, rows + cols - 2)
    with jax.named_scope("first send"):
        send_row(lambda slot: sites.at[0], sites, sites_send, sites_recv, -1)
        send_col(gathered.at[0, 0], gathered.at[0], gather_send.at[0], gather_recv.at[0])

    kinds_packed = jnp.broadcast_to(jnp.concatenate([kinds] * group, axis=1), (nfreq, LANES))
    omega = pick(kinds_packed, omegas, ntypes)
    alpha = pick(kinds_packed, alphas, ntypes)
    ratio = pick(level, frequencies, nfreq) / omega
    diagonal = (1.0 + ratio * ratio) / alpha
    inverse_diagonal = alpha / (1.0 + ratio * ratio)
    zeros_tail = jnp.zeros((nfreq, LANES - 3 * piece), F32)
    start_full = jnp.concatenate([start_packed, zeros_tail], axis=1)
    field_full = jnp.concatenate([packed(field), zeros_tail], axis=1)
    source_full = field_full - diagonal * start_full

    def total_of(values):
        while len(values) > 1:
            values = [sum(values[k:k + 2]) for k in range(0, len(values), 2)]
        return values[0]

    def unpack(block_of, count):
        blocks = [block_of(s) for s in range(count)]
        return [
            jnp.concatenate(
                [
                    jnp.concatenate([blocks[t + q][:, a * piece:(a + 1) * piece] for q in range(group)], axis=1)
                    for t in range(0, count, group)
                ],
                axis=1,
            )
            for a in range(3)
        ]

    def prepare():
        for c in range(cols):
            across = gathered[0, c].T[3 * piece:, :]
            for q in range(4):
                columns[q, c * piece:(c + 1) * piece, :] = jnp.broadcast_to(across[:, q:q + 1], (piece, LANES))
        for r in range(rows):
            own_sites[:, r * piece:(r + 1) * piece] = sites[r][:, 3 * piece:]

    apart = (
        lax.broadcasted_iota(jnp.int32, (piece, LANES), 0) != lax.broadcasted_iota(jnp.int32, (piece, LANES), 1)
    )

    def build(chunk):
        for c in range(cols):
            base = slice(c * piece, (c + 1) * piece)
            column = [columns[q, base, :] for q in range(4)]
            for n in range(depth // LANES):
                span = slice(n * LANES, (n + 1) * LANES)
                place = slice(chunk * depth + n * LANES, chunk * depth + (n + 1) * LANES)
                offset = [column[q] - own_sites[q:q + 1, place] for q in range(3)]
                reach = column[3] + own_sites[3:4, place]
                square = offset[0] * offset[0] + offset[1] * offset[1] + offset[2] * offset[2] + reach * reach
                inverse = lax.rsqrt(square)
                second = inverse * inverse
                cube = second * inverse
                fifth = -3.0 * (cube * second)
                weighted = [offset[q] * fifth for q in range(3)]
                for number, (a, b) in enumerate(PAIRS):
                    value = weighted[a] * offset[b]
                    if a == b:
                        value = value + cube
                    if chunk == 0 and c == 0 and n == 0:
                        value = jnp.where(apart, value, 0.0)
                    high = value.astype(BF16)
                    coupling[chunk, number, 0, base, span] = high
                    coupling[chunk, number, 1, base, span] = (value - high.astype(F32)).astype(BF16)

    def contract(chunk, lefts):
        out = [None] * 3

        def add(a, value):
            out[a] = value if out[a] is None else out[a] + value

        def dot(left, number, part):
            return jnp.dot(left, coupling[chunk, number, part], preferred_element_type=F32)

        for number, (a, b) in enumerate(PAIRS):
            first, second = lefts[number]
            main, rest = dot(first, number, 0), dot(second, number, 1)
            add(a, main[:nfreq] + (main[nfreq:2 * nfreq] + rest[:nfreq]))
            if a != b:
                add(b, main[2 * nfreq:3 * nfreq] + (main[3 * nfreq:] + rest[nfreq:]))
        return out

    def apply(turn):
        with jax.named_scope("gather wait"):
            wait_for(gathered.at[turn], cols - 1, gather_recv.at[turn])
            if turn == 0:
                wait_for(sites, rows - 1, sites_recv)
        outs = [None] * tiles
        with jax.named_scope("contract"):
            if turn == 0:
                prepare()
            values = unpack(lambda s: gathered[turn, s], cols)
            highs = [value.astype(BF16).astype(F32) for value in values]
            lows = [value - high for value, high in zip(values, highs)]
            lefts = []
            for a, b in PAIRS:
                if a == b:
                    main, rest = [highs[a], lows[a]], [highs[a], lows[a]]
                else:
                    main, rest = [highs[b], lows[b], highs[a], lows[a]], [highs[b], highs[a]]
                lefts.append(tuple(jnp.concatenate(part, axis=0).astype(BF16) for part in (main, rest)))
            for chunk in range(tiles - 1, -1, -1):
                if turn == 0:
                    build(chunk)
                out = contract(chunk, lefts)
                outs[chunk] = out
                first = chunk * TILE
                for s in range(TILE):
                    cut = slice(s * piece, (s + 1) * piece)
                    block = jnp.concatenate([out[0][:, cut], out[1][:, cut], out[2][:, cut], zeros_tail], axis=1)
                    if first + s == 0:
                        landed[turn, 0] = block
                    else:
                        partial[turn, first + s] = block
                send_row(
                    lambda slot: partial.at[turn, slot], landed.at[turn], fold_send.at[turn], fold_recv.at[turn], 1,
                    range(first + TILE - 1, max(first - 1, 0), -1),
                )
        return outs

    def folded(turn):
        with jax.named_scope("fold wait"):
            wait_for(landed.at[turn], rows - 1, fold_recv.at[turn])
        return total_of([landed[turn, r] for r in range(rows)])

    def spread(turn, value):
        gathered[turn, 0] = value
        with jax.named_scope("gather send"):
            send_col(gathered.at[turn, 0], gathered.at[turn], gather_send.at[turn], gather_recv.at[turn])

    apply(0)
    powers = [source_full - folded(0)]
    scaled = []
    for turn in range(1, APPLICATIONS - 1):
        scaled.append(powers[-1] * inverse_diagonal)
        spread(turn, scaled[-1])
        apply(turn)
        powers.append(folded(turn))

    last = APPLICATIONS - 1
    scaled.append(powers[-1] * inverse_diagonal)
    spread(last, scaled[-1])
    mates[0] = scaled[-1]
    send_row(lambda slot: mates.at[0], mates, mates_send, mates_recv, -1)
    moments = jnp.zeros((nfreq, LANES), F32)
    for k, (i, j) in enumerate(MOMENTS):
        local = jnp.sum(scaled[i] * powers[j], axis=1, keepdims=True)
        moments = jnp.where(lane == k, local, moments)
    outs = apply(last)
    with jax.named_scope("mates wait"):
        wait_for(mates, rows - 1, mates_recv)
    terms = []
    for chunk in range(tiles):
        own = unpack(lambda s: mates[chunk * TILE + s], TILE)
        terms += [own[a] * outs[chunk][a] for a in range(3)]
    local = jnp.sum(total_of(terms), axis=1, keepdims=True)
    moments = jnp.where(lane == len(MOMENTS), local, moments)
    with jax.named_scope("sum"):
        col_sums[0] = moments
        send_col(col_sums.at[0], col_sums, sum_send.at[0], sum_recv.at[0])
        wait_for(col_sums, cols - 1, sum_recv.at[0])
        row_sums[0] = total_of([col_sums[c] for c in range(cols)])
        send_row(lambda slot: row_sums.at[0], row_sums, sum_send.at[1], sum_recv.at[1], -1)
        powers.append(folded(last))
        wait_for(row_sums, rows - 1, sum_recv.at[1])
    total = total_of([row_sums[r] for r in range(rows)])

    m = [jnp.broadcast_to(total[:, k:k + 1], (nfreq, LANES)) for k in range(6)]
    a0 = m[1] / m[0]
    h0 = m[0]
    h1 = m[2] - a0 * m[1]
    a1 = (m[3] - 2.0 * a0 * m[2] + a0 * a0 * m[1]) / h1
    b1 = h1 / h0
    c1 = -(a0 + a1)
    c0 = a0 * a1 - b1
    h2 = m[4] + c1 * m[3] + c0 * m[2]
    a2 = (m[5] + c1 * m[4] + c0 * m[3]) / h2 + c1
    b2 = h2 / h1
    e2 = c1 - a2
    e1 = c0 - a2 * c1 - b2
    e0 = b2 * a0 - a2 * c0
    top = 1.0 / (e2 - 1.0 - e1 + e0)
    p3, p2, p1, p0 = top, e2 * top, e1 * top, e0 * top
    s2 = -p3
    s1 = -p2 - s2
    s0 = -p1 - s1
    residual = p0 * powers[0] + p1 * powers[1] + p2 * powers[2] + p3 * powers[3]
    dipoles = start_full + (s0 * scaled[0] + s1 * scaled[1] + s2 * scaled[2])
    for a in range(3):
        dipoles_out[a] = dipoles[:, a * piece:(a + 1) * piece]
        residual_out[a] = residual[:, a * piece:(a + 1) * piece]

    for turn in range(APPLICATIONS):
        wait_for(gathered.at[turn], cols - 1, gather_send.at[turn])
        wait_for(landed.at[turn], rows - 1, fold_send.at[turn])
    wait_for(sites, rows - 1, sites_send)
    wait_for(mates, rows - 1, mates_send)
    wait_for(col_sums, cols - 1, sum_send.at[0])
    wait_for(row_sums, rows - 1, sum_send.at[1])


def solution(mesh):
    rows, cols = mesh.shape["row"], mesh.shape["col"]

    def shards(positions, atom_types, alpha_table, omega_table, radius_table, frequencies, field, start_dipoles):
        piece, nfreq = positions.shape[1], frequencies.shape[0]
        side = (10.0 * piece * rows * cols) ** (1.0 / 3.0)
        operands = (
            positions, atom_types.reshape(1, piece), alpha_table, omega_table, radius_table, frequencies,
            field, start_dipoles,
        )
        vmem = pl.BlockSpec(memory_space=pltpu.VMEM)
        tile = (nfreq, LANES)
        dma = pltpu.SemaphoreType.DMA
        places = [pltpu.VMEM] * 2 + [pltpu.SMEM] * 4 + [pltpu.VMEM] * 2
        return pl.pallas_call(
            functools.partial(kernel, rows, cols, piece, side),
            out_shape=(jax.ShapeDtypeStruct(field.shape, F32),) * 2,
            in_specs=[pl.BlockSpec(memory_space=pltpu.HBM)] * len(operands),
            out_specs=(vmem, vmem),
            scratch_shapes=[space(array.shape, array.dtype) for space, array in zip(places, operands)] + [
                pltpu.VMEM((APPLICATIONS, cols) + tile, F32),
                pltpu.VMEM((APPLICATIONS, rows) + tile, F32),
                pltpu.VMEM((APPLICATIONS, rows) + tile, F32),
                pltpu.VMEM((rows,) + tile, F32),
                pltpu.VMEM((rows,) + tile, F32),
                pltpu.VMEM((nfreq, rows * piece), F32),
                pltpu.VMEM((4, cols * piece, LANES), F32),
                pltpu.VMEM((rows // TILE, len(PAIRS), 2, cols * piece, TILE * piece), BF16),
                pltpu.VMEM((cols,) + tile, F32),
                pltpu.VMEM((rows,) + tile, F32),
                dma((len(operands),)),
                dma((APPLICATIONS,)), dma((APPLICATIONS,)),
                dma, dma,
                dma((APPLICATIONS,)), dma((APPLICATIONS,)),
                dma, dma,
                dma((2,)), dma((2,)),
            ],
            compiler_params=pltpu.CompilerParams(
                collective_id=0, has_side_effects=True, vmem_limit_bytes=64 * 1024 * 1024
            ),
        )(*operands)

    placed = (
        P(None, ("row", "col")),
        P(("row", "col")),
        P(),
        P(),
        P(),
        P(),
        P(None, None, ("row", "col")),
        P(None, None, ("row", "col")),
    )
    return jax.shard_map(
        shards,
        mesh=mesh,
        in_specs=placed,
        out_specs=(P(None, None, ("row", "col")), P(None, None, ("row", "col"))),
        check_vma=False,
    )
```

time: 85.5 us -> 77.8 us (0.910)
  Pallas kernels: 82.7 us -> 75 us
    pallas_call x1, Pallas kernels: 82.7 us -> 75 us  [shards(): pl.pallas_call(functools.partial(kernel, rows, cols, piece, side), out_sh...]
where the time goes in v3:
time: 77.8 us; the launch traced here: 77.6 us
  Pallas kernels  75 us (96%)
  local copies, waits for them, and re-layouts  1.92 us (2%)
    pallas_call x1, Pallas kernels, shards(): pl.pallas_call(functools.partial(kernel, rows, cols, piece, side), out_sh...  75 us
    unnamed x4, local copies, waits for them, and re-layouts  1.92 us

profile of v3, /device:TPU:1, one launch (start us, length us, event | category | flops | bytes accessed | tf_op | source)
XLA Modules:
  0.0 77.6 jit_solution(15889797627829663908)
XLA Ops:
  0.6 75.0 %shard_map.95 = (f32[3,8,32]{2,1,0:T(8,128)}, f32[3,8,32]{2,1,0:T(8,128)}) custom-call(f32[3,32]{1,0:T(4,128)} %positions_hbm.1, s32[1,32]{1,0:T(1,128)} %bitcast.1, f32[5]{0:T(128)} %alphas_hbm.1, f32[5]{0:T(128)} %omegas_hbm.1, f32[5]{0:T(128)} %radii_hbm.1, f32[8]{0:T(128)} %frequencies_hbm.1, f32[3,8,32]{2,1,0:T(8,128)} %field_hbm.1, f32[3,8,32]{2,1,0:T(8,128)} %start_hbm.1), custom_call_target="tpu_custom_call" | custom-call | tf_op jit(solution)/shard_map/pallas_call | solution.py:352
  75.6 0.0 copy-start
  75.6 1.3 %copy.12 = f32[3,8,32]{2,1,0:T(8,128)} copy(f32[3,8,32]{2,1,0:T(8,128)} %get-tuple-element.4) | data formatting | bytes 6144
  77.0 0.0 copy-done
  77.0 0.6 copy.13
Async XLA Ops:
  75.6 1.3 %copy-start = (f32[3,8,32]{2,1,0:T(8,128)S(1)}, f32[3,8,32]{2,1,0:T(8,128)}, u32[]{:S(2)}) copy-start(f32[3,8,32]{2,1,0:T(8,128)} %get-tuple-element.5) | copy-start | bytes 9220

commit v4 on v3

--- a/solution.py
+++ b/solution.py
@@ -13,6 +13,7 @@
 PAIRS = ((0, 0), (1, 1), (2, 2), (0, 1), (0, 2), (1, 2))
 LANES = 128
 TILE = 8
+SHORT = 6
 ROW_MINOR = 4
 COL_MINOR = 2
 MOMENTS = ((0, 0), (0, 1), (1, 1), (1, 2), (2, 2))
@@ -46,7 +47,7 @@
 def kernel(
     rows, cols, piece, side,
     positions_hbm, types_hbm, alphas_hbm, omegas_hbm, radii_hbm, frequencies_hbm, field_hbm, start_hbm,
-    dipoles_out, residual_out,
+    out_ref,
     positions, types, alphas, omegas, radii, frequencies, field, start,
     gathered, partial, landed, sites, mates, own_sites, columns, coupling, col_sums, row_sums,
     load_sem, gather_send, gather_recv, sites_send, sites_recv, fold_send, fold_recv,
@@ -92,10 +93,11 @@
     for load in loads:
         load.start()
 
-    def send_row(source_of, target, send_sem, recv_sem, sign, slots=row_order):
+    def send_row(source_of, target, send_sem, recv_sem, sign, slots=row_order, height=None):
         for slot in slots:
             pltpu.make_async_remote_copy(
-                src_ref=source_of(slot), dst_ref=target.at[slot], send_sem=send_sem, recv_sem=recv_sem,
+                src_ref=source_of(slot), dst_ref=target.at[slot] if height is None else target.at[slot, pl.ds(0, height)],
+                send_sem=send_sem, recv_sem=recv_sem,
                 device_id=row_peer(slot, sign), device_id_type=MESH,
             ).start()
 
@@ -106,8 +108,8 @@
                 device_id=col_peer(slot, -1), device_id_type=MESH,
             ).start()
 
-    def wait_for(buffer, count, sem):
-        view = buffer.at[pl.ds(0, count)]
+    def wait_for(buffer, count, sem, height=None):
+        view = buffer.at[pl.ds(0, count)] if height is None else buffer.at[pl.ds(0, count), pl.ds(0, height)]
         pltpu.make_async_copy(view, view, sem).wait()
 
     def packed(ref):
@@ -241,23 +243,31 @@
                 out = contract(chunk, lefts)
                 outs[chunk] = out
                 first = chunk * TILE
+                low = jnp.concatenate([out[a][SHORT:] for a in range(3)] + [out[0][SHORT:]], axis=0)
                 for s in range(TILE):
                     cut = slice(s * piece, (s + 1) * piece)
-                    block = jnp.concatenate([out[0][:, cut], out[1][:, cut], out[2][:, cut], zeros_tail], axis=1)
+                    block = jnp.concatenate([out[0][:, cut], out[1][:, cut], out[2][:, cut], low[:, cut]], axis=1)
                     if first + s == 0:
                         landed[turn, 0] = block
                     else:
                         partial[turn, first + s] = block
                 send_row(
-                    lambda slot: partial.at[turn, slot], landed.at[turn], fold_send.at[turn], fold_recv.at[turn], 1,
-                    range(first + TILE - 1, max(first - 1, 0), -1),
+                    lambda slot: partial.at[turn, slot, pl.ds(0, SHORT)], landed.at[turn], fold_send.at[turn],
+                    fold_recv.at[turn], 1, range(first + TILE - 1, max(first - 1, 0), -1), SHORT,
                 )
         return outs
 
     def folded(turn):
         with jax.named_scope("fold wait"):
-            wait_for(landed.at[turn], rows - 1, fold_recv.at[turn])
-        return total_of([landed[turn, r] for r in range(rows)])
+            wait_for(landed.at[turn], rows - 1, fold_recv.at[turn], SHORT)
+        total = total_of([landed[turn, r, :SHORT] for r in range(rows)])
+        parts = [
+            jnp.concatenate(
+                [total[:, a * piece:(a + 1) * piece], total[a * (nfreq - SHORT):(a + 1) * (nfreq - SHORT), 3 * piece:]], axis=0
+            )
+            for a in range(3)
+        ]
+        return jnp.concatenate(parts + [zeros_tail], axis=1)
 
     def spread(turn, value):
         gathered[turn, 0] = value
@@ -292,16 +302,18 @@
     local = jnp.sum(total_of(terms), axis=1, keepdims=True)
     moments = jnp.where(lane == len(MOMENTS), local, moments)
     with jax.named_scope("sum"):
-        col_sums[0] = moments
+        spaced = pltpu.roll(moments, 0, 1, stride=LANES // nfreq, stride_axis=0)
+        col_sums[0] = jnp.sum(spaced, axis=0, keepdims=True)
         send_col(col_sums.at[0], col_sums, sum_send.at[0], sum_recv.at[0])
         wait_for(col_sums, cols - 1, sum_recv.at[0])
         row_sums[0] = total_of([col_sums[c] for c in range(cols)])
         send_row(lambda slot: row_sums.at[0], row_sums, sum_send.at[1], sum_recv.at[1], -1)
         powers.append(folded(last))
         wait_for(row_sums, rows - 1, sum_recv.at[1])
-    total = total_of([row_sums[r] for r in range(rows)])
-
-    m = [jnp.broadcast_to(total[:, k:k + 1], (nfreq, LANES)) for k in range(6)]
+    total = jnp.broadcast_to(total_of([row_sums[r] for r in range(rows)]), (nfreq, LANES))
+    column_of = lane - level * (LANES // nfreq)
+
+    m = [jnp.sum(jnp.where(column_of == k, total, 0.0), axis=1, keepdims=True) for k in range(len(MOMENTS) + 1)]
     a0 = m[1] / m[0]
     h0 = m[0]
     h1 = m[2] - a0 * m[1]
@@ -323,12 +335,12 @@
     residual = p0 * powers[0] + p1 * powers[1] + p2 * powers[2] + p3 * powers[3]
     dipoles = start_full + (s0 * scaled[0] + s1 * scaled[1] + s2 * scaled[2])
     for a in range(3):
-        dipoles_out[a] = dipoles[:, a * piece:(a + 1) * piece]
-        residual_out[a] = residual[:, a * piece:(a + 1) * piece]
+        out_ref[0, a] = dipoles[:, a * piece:(a + 1) * piece]
+        out_ref[1, a] = residual[:, a * piece:(a + 1) * piece]
 
     for turn in range(APPLICATIONS):
         wait_for(gathered.at[turn], cols - 1, gather_send.at[turn])
-        wait_for(landed.at[turn], rows - 1, fold_send.at[turn])
+        wait_for(landed.at[turn], rows - 1, fold_send.at[turn], SHORT)
     wait_for(sites, rows - 1, sites_send)
     wait_for(mates, rows - 1, mates_send)
     wait_for(col_sums, cols - 1, sum_send.at[0])
@@ -349,11 +361,11 @@
         tile = (nfreq, LANES)
         dma = pltpu.SemaphoreType.DMA
         places = [pltpu.VMEM] * 2 + [pltpu.SMEM] * 4 + [pltpu.VMEM] * 2
-        return pl.pallas_call(
+        both = pl.pallas_call(
             functools.partial(kernel, rows, cols, piece, side),
-            out_shape=(jax.ShapeDtypeStruct(field.shape, F32),) * 2,
+            out_shape=jax.ShapeDtypeStruct((2,) + field.shape, F32),
             in_specs=[pl.BlockSpec(memory_space=pltpu.HBM)] * len(operands),
-            out_specs=(vmem, vmem),
+            out_specs=vmem,
             scratch_shapes=[space(array.shape, array.dtype) for space, array in zip(places, operands)] + [
                 pltpu.VMEM((APPLICATIONS, cols) + tile, F32),
                 pltpu.VMEM((APPLICATIONS, rows) + tile, F32),
@@ -363,8 +375,8 @@
                 pltpu.VMEM((nfreq, rows * piece), F32),
                 pltpu.VMEM((4, cols * piece, LANES), F32),
                 pltpu.VMEM((rows // TILE, len(PAIRS), 2, cols * piece, TILE * piece), BF16),
-                pltpu.VMEM((cols,) + tile, F32),
-                pltpu.VMEM((rows,) + tile, F32),
+                pltpu.VMEM((cols, 1, LANES), F32),
+                pltpu.VMEM((rows, 1, LANES), F32),
                 dma((len(operands),)),
                 dma((APPLICATIONS,)), dma((APPLICATIONS,)),
                 dma, dma,
@@ -376,6 +388,7 @@
                 collective_id=0, has_side_effects=True, vmem_limit_bytes=64 * 1024 * 1024
             ),
         )(*operands)
+        return both[0], both[1]
 
     placed = (
         P(None, ("row", "col")),

time: 77.8 us -> 76.1 us (0.978)
  Pallas kernels: 75 us -> 73.9 us
    unnamed x4 -> x0, local copies, waits for them, and re-layouts: 1.92 us -> none
    squeeze x0 -> x1, local copies, waits for them, and re-layouts: none -> 1.33 us  [shards(): return (both[0], both[1])]
    pallas_call x1, Pallas kernels: 75 us -> 73.9 us  [shards(): pl.pallas_call(functools.partial(kernel, rows, cols, piece, side), out_sh...]
where the time goes in v4:
time: 76.1 us; the launch traced here: 75.9 us
  Pallas kernels  73.9 us (97%)
  local copies, waits for them, and re-layouts  1.33 us (2%)
    pallas_call x1, Pallas kernels, shards(): pl.pallas_call(functools.partial(kernel, rows, cols, piece, side), out_sh...  73.9 us

profile of v4, /device:TPU:1, one launch (start us, length us, event | category | flops | bytes accessed | tf_op | source)
XLA Modules:
  0.0 75.9 jit_solution(10772991375033952991)
XLA Ops:
  0.6 73.9 %shard_map.95 = f32[2,3,8,32]{3,2,1,0:T(8,128)} custom-call(f32[3,32]{1,0:T(4,128)} %positions_hbm.1, s32[1,32]{1,0:T(1,128)} %bitcast.5, f32[5]{0:T(128)} %alphas_hbm.1, f32[5]{0:T(128)} %omegas_hbm.1, f32[5]{0:T(128)} %radii_hbm.1, f32[8]{0:T(128)} %frequencies_hbm.1, f32[3,8,32]{2,1,0:T(8,128)} %field_hbm.1, f32[3,8,32]{2,1,0:T(8,128)} %start_hbm.1), custom_call_target="tpu_custom_call" | custom-call | tf_op jit(solution)/shard_map/pallas_call | solution.py:364
  74.5 1.3 %slice_bitcast_fusion = (f32[3,8,32]{2,1,0:T(8,128)}, f32[3,8,32]{2,1,0:T(8,128)}) fusion(f32[2,3,8,32]{3,2,1,0:T(8,128)} %shard_map.95), kind=kLoop, calls=%fused_computation | loop fusion | bytes 12288 | tf_op jit(solution)/shard_map/squeeze | solution.py:391

commit v5 on v4

--- a/solution.py
+++ b/solution.py
@@ -16,6 +16,7 @@
 SHORT = 6
 ROW_MINOR = 4
 COL_MINOR = 2
+COL_FIRST = 1
 MOMENTS = ((0, 0), (0, 1), (1, 1), (1, 2), (2, 2))
 
 
@@ -84,11 +85,17 @@
     row_order = range(rows - 1, 0, -1)
     col_order = range(cols - 1, 0, -1)
 
+    reach_row = [hops(far, len(row_high)) + hops(near, len(row_low)) for far, near in row_offsets]
+    reach_col = [hops(far, len(col_high)) for far, _ in col_offsets]
+    everyone = sorted(
+        [(-reach_row[slot], False, -slot) for slot in row_order]
+        + [(-reach_col[slot] - COL_FIRST, True, -slot) for slot in col_order]
+    )
+
     with jax.named_scope("greet"):
-        for slot in row_order:
-            pl.semaphore_signal(barrier, inc=1, device_id=row_peer(slot, 1), device_id_type=MESH)
-        for slot in col_order:
-            pl.semaphore_signal(barrier, inc=1, device_id=col_peer(slot, 1), device_id_type=MESH)
+        for _, along_col, slot in everyone:
+            peer = col_peer(-slot, 1) if along_col else row_peer(-slot, 1)
+            pl.semaphore_signal(barrier, inc=1, device_id=peer, device_id_type=MESH)
 
     for load in loads:
         load.start()
@@ -101,8 +108,8 @@
                 device_id=row_peer(slot, sign), device_id_type=MESH,
             ).start()
 
-    def send_col(source, target, send_sem, recv_sem):
-        for slot in col_order:
+    def send_col(source, target, send_sem, recv_sem, slots=col_order):
+        for slot in slots:
             pltpu.make_async_remote_copy(
                 src_ref=source, dst_ref=target.at[slot], send_sem=send_sem, recv_sem=recv_sem,
                 device_id=col_peer(slot, -1), device_id_type=MESH,
@@ -132,8 +139,11 @@
     with jax.named_scope("barrier"):
         pl.semaphore_wait(barrier, rows + cols - 2)
     with jax.named_scope("first send"):
-        send_row(lambda slot: sites.at[0], sites, sites_send, sites_recv, -1)
-        send_col(gathered.at[0, 0], gathered.at[0], gather_send.at[0], gather_recv.at[0])
+        for _, along_col, slot in everyone:
+            if along_col:
+                send_col(gathered.at[0, 0], gathered.at[0], gather_send.at[0], gather_recv.at[0], (-slot,))
+            else:
+                send_row(lambda _: sites.at[0, pl.ds(0, 4)], sites, sites_send, sites_recv, -1, (-slot,), 4)
 
     kinds_packed = jnp.broadcast_to(jnp.concatenate([kinds] * group, axis=1), (nfreq, LANES))
     omega = pick(kinds_packed, omegas, ntypes)
@@ -169,8 +179,10 @@
             across = gathered[0, c].T[3 * piece:, :]
             for q in range(4):
                 columns[q, c * piece:(c + 1) * piece, :] = jnp.broadcast_to(across[:, q:q + 1], (piece, LANES))
+
+    def place_sites():
         for r in range(rows):
-            own_sites[:, r * piece:(r + 1) * piece] = sites[r][:, 3 * piece:]
+            own_sites[:, r * piece:(r + 1) * piece] = sites[r, :4, 3 * piece:]
 
     apart = (
         lax.broadcasted_iota(jnp.int32, (piece, LANES), 0) != lax.broadcasted_iota(jnp.int32, (piece, LANES), 1)
@@ -221,12 +233,13 @@
     def apply(turn):
         with jax.named_scope("gather wait"):
             wait_for(gathered.at[turn], cols - 1, gather_recv.at[turn])
-            if turn == 0:
-                wait_for(sites, rows - 1, sites_recv)
+        if turn == 0:
+            prepare()
+            with jax.named_scope("sites wait"):
+                wait_for(sites, rows - 1, sites_recv, 4)
+            place_sites()
         outs = [None] * tiles
         with jax.named_scope("contract"):
-            if turn == 0:
-                prepare()
             values = unpack(lambda s: gathered[turn, s], cols)
             highs = [value.astype(BF16).astype(F32) for value in values]
             lows = [value - high for value, high in zip(values, highs)]
@@ -341,7 +354,7 @@
     for turn in range(APPLICATIONS):
         wait_for(gathered.at[turn], cols - 1, gather_send.at[turn])
         wait_for(landed.at[turn], rows - 1, fold_send.at[turn], SHORT)
-    wait_for(sites, rows - 1, sites_send)
+    wait_for(sites, rows - 1, sites_send, 4)
     wait_for(mates, rows - 1, mates_send)
     wait_for(col_sums, cols - 1, sum_send.at[0])
     wait_for(row_sums, rows - 1, sum_send.at[1])
@@ -372,7 +385,7 @@
                 pltpu.VMEM((APPLICATIONS, rows) + tile, F32),
                 pltpu.VMEM((rows,) + tile, F32),
                 pltpu.VMEM((rows,) + tile, F32),
-                pltpu.VMEM((nfreq, rows * piece), F32),
+                pltpu.VMEM((4, rows * piece), F32),
                 pltpu.VMEM((4, cols * piece, LANES), F32),
                 pltpu.VMEM((rows // TILE, len(PAIRS), 2, cols * piece, TILE * piece), BF16),
                 pltpu.VMEM((cols, 1, LANES), F32),

time: 76.1 us -> 75.1 us (0.987)
  Pallas kernels: 73.9 us -> 72.9 us
    pallas_call x1, Pallas kernels: 73.9 us -> 72.9 us  [shards(): pl.pallas_call(functools.partial(kernel, rows, cols, piece, side), out_sh...]
where the time goes in v5:
time: 75.1 us; the launch traced here: 74.9 us
  Pallas kernels  72.9 us (97%)
  local copies, waits for them, and re-layouts  1.33 us (2%)
    pallas_call x1, Pallas kernels, shards(): pl.pallas_call(functools.partial(kernel, rows, cols, piece, side), out_sh...  72.9 us

profile of v5, /device:TPU:1, one launch (start us, length us, event | category | flops | bytes accessed | tf_op | source)
XLA Modules:
  0.0 74.9 jit_solution(14637272728105671014)
XLA Ops:
  0.6 72.9 %shard_map.95 = f32[2,3,8,32]{3,2,1,0:T(8,128)} custom-call(f32[3,32]{1,0:T(4,128)} %positions_hbm.1, s32[1,32]{1,0:T(1,128)} %bitcast.5, f32[5]{0:T(128)} %alphas_hbm.1, f32[5]{0:T(128)} %omegas_hbm.1, f32[5]{0:T(128)} %radii_hbm.1, f32[8]{0:T(128)} %frequencies_hbm.1, f32[3,8,32]{2,1,0:T(8,128)} %field_hbm.1, f32[3,8,32]{2,1,0:T(8,128)} %start_hbm.1), custom_call_target="tpu_custom_call" | custom-call | tf_op jit(solution)/shard_map/pallas_call | solution.py:377
  73.5 1.3 %slice_bitcast_fusion = (f32[3,8,32]{2,1,0:T(8,128)}, f32[3,8,32]{2,1,0:T(8,128)}) fusion(f32[2,3,8,32]{3,2,1,0:T(8,128)} %shard_map.95), kind=kLoop, calls=%fused_computation | loop fusion | bytes 12288 | tf_op jit(solution)/shard_map/squeeze | solution.py:404

commit v6 on v5

--- a/solution.py
+++ b/solution.py
@@ -376,7 +376,7 @@
         places = [pltpu.VMEM] * 2 + [pltpu.SMEM] * 4 + [pltpu.VMEM] * 2
         both = pl.pallas_call(
             functools.partial(kernel, rows, cols, piece, side),
-            out_shape=jax.ShapeDtypeStruct((2,) + field.shape, F32),
+            out_shape=pltpu.VMEM((2,) + field.shape, F32),
             in_specs=[pl.BlockSpec(memory_space=pltpu.HBM)] * len(operands),
             out_specs=vmem,
             scratch_shapes=[space(array.shape, array.dtype) for space, array in zip(places, operands)] + [
@@ -398,7 +398,7 @@
                 dma((2,)), dma((2,)),
             ],
             compiler_params=pltpu.CompilerParams(
-                collective_id=0, has_side_effects=True, vmem_limit_bytes=64 * 1024 * 1024
+                collective_id=0, has_side_effects=True, vmem_limit_bytes=60 * 1024 * 1024
             ),
         )(*operands)
         return both[0], both[1]

time: 75.1 us -> 73.7 us (0.981)
  no operation moved by 1% of the time
where the time goes in v6:
time: 73.7 us; the launch traced here: 73.5 us
  Pallas kernels  72.2 us (98%)
    pallas_call x1, Pallas kernels, shards(): pl.pallas_call(functools.partial(kernel, rows, cols, piece, side), out_sh...  72.2 us

profile of v6, /device:TPU:1, one launch (start us, length us, event | category | flops | bytes accessed | tf_op | source)
XLA Modules:
  0.0 73.5 jit_solution(16160873374656318455)
XLA Ops:
  0.6 72.2 %shard_map.95 = f32[2,3,8,32]{3,2,1,0:T(8,128)S(1)} custom-call(f32[3,32]{1,0:T(4,128)} %positions_hbm.1, s32[1,32]{1,0:T(1,128)} %bitcast.5, f32[5]{0:T(128)} %alphas_hbm.1, f32[5]{0:T(128)} %omegas_hbm.1, f32[5]{0:T(128)} %radii_hbm.1, f32[8]{0:T(128)} %frequencies_hbm.1, f32[3,8,32]{2,1,0:T(8,128)} %field_hbm.1, f32[3,8,32]{2,1,0:T(8,128)} %start_hbm.1), custom_call_target="tpu_custom_call" | custom-call | tf_op jit(solution)/shard_map/pallas_call | solution.py:377
  72.9 0.6 slice_bitcast_fusion

commit v7 on v6

--- a/solution.py
+++ b/solution.py
@@ -230,6 +230,21 @@
                 add(b, main[2 * nfreq:3 * nfreq] + (main[3 * nfreq:] + rest[nfreq:]))
         return out
 
+    def send_chunk(turn, chunk, out):
+        first = chunk * TILE
+        low = jnp.concatenate([out[a][SHORT:] for a in range(3)] + [out[0][SHORT:]], axis=0)
+        for s in range(TILE):
+            cut = slice(s * piece, (s + 1) * piece)
+            block = jnp.concatenate([out[0][:, cut], out[1][:, cut], out[2][:, cut], low[:, cut]], axis=1)
+            if first + s == 0:
+                landed[turn, 0] = block
+            else:
+                partial[turn, first + s] = block
+        send_row(
+            lambda slot: partial.at[turn, slot, pl.ds(0, SHORT)], landed.at[turn], fold_send.at[turn],
+            fold_recv.at[turn], 1, range(first + TILE - 1, max(first - 1, 0), -1), SHORT,
+        )
+
     def apply(turn):
         with jax.named_scope("gather wait"):
             wait_for(gathered.at[turn], cols - 1, gather_recv.at[turn])
@@ -253,21 +268,13 @@
             for chunk in range(tiles - 1, -1, -1):
                 if turn == 0:
                     build(chunk)
-                out = contract(chunk, lefts)
-                outs[chunk] = out
-                first = chunk * TILE
-                low = jnp.concatenate([out[a][SHORT:] for a in range(3)] + [out[0][SHORT:]], axis=0)
-                for s in range(TILE):
-                    cut = slice(s * piece, (s + 1) * piece)
-                    block = jnp.concatenate([out[0][:, cut], out[1][:, cut], out[2][:, cut], low[:, cut]], axis=1)
-                    if first + s == 0:
-                        landed[turn, 0] = block
-                    else:
-                        partial[turn, first + s] = block
-                send_row(
-                    lambda slot: partial.at[turn, slot, pl.ds(0, SHORT)], landed.at[turn], fold_send.at[turn],
-                    fold_recv.at[turn], 1, range(first + TILE - 1, max(first - 1, 0), -1), SHORT,
-                )
+                if 0 < turn < APPLICATIONS - 1 and chunk >= tiles - 1:
+                    @pl.when(row >= 0)
+                    def _():
+                        send_chunk(turn, chunk, contract(chunk, lefts))
+                else:
+                    outs[chunk] = contract(chunk, lefts)
+                    send_chunk(turn, chunk, outs[chunk])
         return outs
 
     def folded(turn):

time: 73.7 us -> 73.9 us (level)
  no operation moved by 1% of the time
where the time goes in v7:
time: 73.9 us; the launch traced here: 73.8 us
  Pallas kernels  72.5 us (98%)
    pallas_call x1, Pallas kernels, shards(): pl.pallas_call(functools.partial(kernel, rows, cols, piece, side), out_sh...  72.5 us

profile of v7, /device:TPU:1, one launch (start us, length us, event | category | flops | bytes accessed | tf_op | source)
XLA Modules:
  0.0 73.8 jit_solution(13805688072870822209)
XLA Ops:
  0.6 72.5 %shard_map.95 = f32[2,3,8,32]{3,2,1,0:T(8,128)S(1)} custom-call(f32[3,32]{1,0:T(4,128)} %positions_hbm.1, s32[1,32]{1,0:T(1,128)} %bitcast.5, f32[5]{0:T(128)} %alphas_hbm.1, f32[5]{0:T(128)} %omegas_hbm.1, f32[5]{0:T(128)} %radii_hbm.1, f32[8]{0:T(128)} %frequencies_hbm.1, f32[3,8,32]{2,1,0:T(8,128)} %field_hbm.1, f32[3,8,32]{2,1,0:T(8,128)} %start_hbm.1), custom_call_target="tpu_custom_call" | custom-call | tf_op jit(solution)/shard_map/pallas_call | solution.py:384
  73.2 0.6 slice_bitcast_fusion
